TPU v7x, 128 devices: a whole 4x4x4 slice. The times are simulated.
128 devices in a mesh: space: 8 (over y_hi, x), chan: 16 (over z, y_lo, core).
Axes of the slice: x: 4, y: 4 (y_hi: 2, y_lo: 2; y = y_hi * 2 + y_lo), z: 4, core: 2. Of those that a mesh axis runs over, the one named last changes fastest.
Arguments:
- layer_input: bfloat16 [8, 16, 256, 128], P('space', None, 'chan'), may hold values from -6 to 6
- pre_act: bfloat16 [8, 16, 256, 128], P('space', None, 'chan'), may hold values from -8 to 8
- out_grad: bfloat16 [8, 16, 256, 128], P('space', None, 'chan'), may hold values from -6 to 6
- weight_one: bfloat16 [27, 256, 256], P(None, 'chan'), may hold values from -0.078125 to 0.078125
- weight_two: bfloat16 [27, 256, 256], P(None, 'chan'), may hold values from -0.078125 to 0.078125
Outputs:
- input_grad: bfloat16 [8, 16, 256, 128], P('space', None, 'chan')
- grad_one: float32 [27, 256, 256], P(None, 'chan', 'space')
- grad_two: float32 [27, 256, 256], P(None, 'chan', 'space')
All inputs are finite; a program needn't handle non-finite values.
Results may differ from a plain program's by a relative error of at most 0.0049.
Values may be sent and summed in bfloat16 or wider, within the bound.
A program may use at most 64 MiB of HBM per device.

v0:
```python
import jax
import jax.numpy as jnp
from jax import lax
from jax.sharding import PartitionSpec as P


def extended(block, sides, width):
    for axis, dim in sides:
        count = lax.axis_size(axis)
        forward = [(i, i + 1) for i in range(count - 1)]
        backward = [(target, source) for source, target in forward]
        low = lax.ppermute(
            lax.slice_in_dim(block, block.shape[dim] - width, None, axis=dim), axis, forward
        )
        high = lax.ppermute(lax.slice_in_dim(block, 0, width, axis=dim), axis, backward)
        block = jnp.concatenate([low, block, high], axis=dim)
    return block


def silu_slope(value):
    sig = jax.nn.sigmoid(value)
    return sig * (1.0 + value * (1.0 - sig))


def pad_sides(field):
    return jnp.pad(field, ((0, 0), (1, 1), (0, 0), (1, 1)))


def input_rim(field):
    return extended(pad_sides(field), (("space", 0),), 1)


def cotangent_wide(field):
    whole = lax.all_gather(field, "chan", axis=2, tiled=True)
    padded = extended(pad_sides(whole), (("space", 0),), 1)
    return padded


def layer_grads(in_pad, grad_pad, weight):
    depth = grad_pad.shape[0] - 2
    rows_z = grad_pad.shape[1] - 2
    rows_y = grad_pad.shape[3] - 2
    own = in_pad.shape[2]
    grad_core = grad_pad[1:-1, 1:-1, :, 1:-1]
    weight_grads = []
    result = jnp.zeros((depth, rows_z, own, rows_y), jnp.float32)
    index = 0
    for shift_x in range(-1, 2):
        for shift_y in range(-1, 2):
            for shift_z in range(-1, 2):
                window = in_pad[
                    1 + shift_x : 1 + shift_x + depth,
                    1 + shift_z : 1 + shift_z + rows_z,
                    :,
                    1 + shift_y : 1 + shift_y + rows_y,
                ]
                weight_grads.append(
                    lax.dot_general(
                        window,
                        grad_core,
                        (((0, 1, 3), (0, 1, 3)), ((), ())),
                        preferred_element_type=jnp.float32,
                    )
                )
                back = grad_pad[
                    1 - shift_x : 1 - shift_x + depth,
                    1 - shift_z : 1 - shift_z + rows_z,
                    :,
                    1 - shift_y : 1 - shift_y + rows_y,
                ]
                result = result + jnp.einsum(
                    "xzoy,io->xziy", back, weight[index], preferred_element_type=jnp.float32
                )
                index += 1
    return (result, jnp.stack(weight_grads))


def weight_total(partial_value):
    return lax.psum_scatter(partial_value, "space", scatter_dimension=2, tiled=True)


def shards(layer_input, pre_act, out_grad, weight_one, weight_two):
    depth, rows_z, rows_y = (layer_input.shape[0], layer_input.shape[1], layer_input.shape[3])
    scale = float(depth * lax.axis_size("space") * rows_y * rows_z) ** (-0.5)
    pre_float = pre_act.astype(jnp.float32)
    hidden = jax.nn.silu(pre_float).astype(jnp.bfloat16)
    hidden_grad, partial_two = layer_grads(input_rim(hidden), cotangent_wide(out_grad), weight_two)
    summed_two = weight_total(partial_two)
    pre_grad = (hidden_grad * silu_slope(pre_float)).astype(jnp.bfloat16)
    input_grad, partial_one = layer_grads(
        input_rim(layer_input), cotangent_wide(pre_grad), weight_one
    )
    summed_one = weight_total(partial_one)
    return (input_grad.astype(jnp.bfloat16), summed_one * scale, summed_two * scale)


def solution(mesh):
    return jax.shard_map(
        shards,
        mesh=mesh,
        in_specs=(
            P("space", None, "chan", None),
            P("space", None, "chan", None),
            P("space", None, "chan", None),
            P(None, "chan", None),
            P(None, "chan", None),
        ),
        out_specs=(
            P("space", None, "chan", None),
            P(None, "chan", "space"),
            P(None, "chan", "space"),
        ),
        check_vma=False,
    )
```

profile of v0, /device:TPU:1, one launch (start us, length us, event | category | flops | bytes accessed | tf_op | source)
XLA Modules:
  0.0 308.1 jit_solution(15260791088411973139)
XLA Ops:
  8.9 4.0 %collective-permute-start.4 = (bf16[1,18,16,130]{3,2,1,0:T(8,128)(2,1)S(1)}, bf16[1,18,16,130]{3,2,1,0:T(8,128)(2,1)S(1)}, u32[]{:S(2)}, u32[]{:S(2)}) collective-permute-start(bf16[1,18,16,130]{3,2,1,0:T(8,128)(2,1)S(1)} %pad.16), channel_id=1, source_target_pairs={{0,16},{16,32},{32,48},{48,64},{64,80},{80,96},{96,112},{1,17},{17... | collective-permute-start | bytes 224648 | tf_op jit(solution)/shard_map/ppermute | solution.py:12
  12.9 1.3 collective-permute-start.5
  15.2 4.0 %collective-permute-start.6 = (bf16[1,18,16,130]{3,2,1,0:T(8,128)(2,1)S(1)}, bf16[1,18,16,130]{3,2,1,0:T(8,128)(2,1)S(1)}, u32[]{:S(2)}, u32[]{:S(2)}) collective-permute-start(bf16[1,18,16,130]{3,2,1,0:T(8,128)(2,1)S(1)} %pad.17), channel_id=1, source_target_pairs={{0,16},{16,32},{32,48},{48,64},{64,80},{80,96},{96,112},{1,17},{17... | collective-permute-start | bytes 224648 | tf_op jit(solution)/shard_map/ppermute | solution.py:12
  19.2 1.3 collective-permute-start.7
  20.5 28.9 %all-gather.3.cloned.1.call-done = bf16[1,16,256,128]{3,2,1,0:T(8,128)(2,1)} async-done(((bf16[1,16,16,128]{3,2,1,0:T(8,128)(2,1)}), bf16[1,16,256,128]{3,2,1,0:T(8,128)(2,1)}) %all-gather.3.cloned.1.call-update) | async-done | bytes 1048592 | tf_op jit(solution)/shard_map/all_gather | solution.py:34
  49.4 1.5 copy.88
  53.6 4.1 %collective-permute-start.1 = (bf16[1,18,256,130]{2,3,1,0:T(8,128)(2,1)S(1)}, bf16[1,18,256,130]{2,3,1,0:T(8,128)(2,1)S(1)}, u32[]{:S(2)}, u32[]{:S(2)}) collective-permute-start(bf16[1,18,256,130]{2,3,1,0:T(8,128)(2,1)S(1)} %pad.14.clone), channel_id=1, source_target_pairs={{0,16},{16,32},{32,48},{48,64},{64,80},{80,96},{96,112},{1,17},{17... | collective-permute-start | bytes 3594248 | tf_op jit(solution)/shard_map/ppermute | solution.py:12
  66.3 15.8 %collective-permute-done = bf16[1,18,256,130]{2,3,1,0:T(8,128)(2,1)S(1)} collective-permute-done((bf16[1,18,256,130]{2,3,1,0:T(8,128)(2,1)S(1)}, bf16[1,18,256,130]{2,3,1,0:T(8,128)(2,1)S(1)}, u32[]{:S(2)}, u32[]{:S(2)}) %collective-permute-start) | collective-permute-done | bytes 1198112 | tf_op jit(solution)/shard_map/ppermute | solution.py:15
  94.7 4.3 %copy.50 = f32[27,16,256]{1,0,2:T(8,128)} copy(f32[27,16,256]{2,1,0:T(8,128)S(1)} %fusion.51) | data formatting | bytes 884736
  99.1 4.7 %reshape.688 = f32[256,432]{1,0:T(8,128)} reshape(f32[256,27,16]{2,1,0:T(8,128)} %bitcast.1189) | data formatting | bytes 884736
  103.8 24.3 %all-gather.5.cloned.1.call-done = bf16[1,16,256,128]{3,2,1,0:T(8,128)(2,1)} async-done(((bf16[1,16,16,128]{3,2,1,0:T(8,128)(2,1)}), bf16[1,16,256,128]{3,2,1,0:T(8,128)(2,1)}) %all-gather.5.cloned.1.call-update) | async-done | bytes 1048592 | tf_op jit(solution)/shard_map/all_gather | solution.py:34
  128.2 1.5 copy.89
  129.7 1.5 pad.15.clone
  143.2 4.3 %copy.48 = f32[27,16,256]{1,0,2:T(8,128)} copy(f32[27,16,256]{2,1,0:T(8,128)S(1)} %fusion.78) | data formatting | bytes 884736
  147.6 4.7 %reshape.686 = f32[256,432]{1,0:T(8,128)} reshape(f32[256,27,16]{2,1,0:T(8,128)} %bitcast.1190) | data formatting | bytes 884736
  152.3 52.7 %reduce-scatter.9.cloned.1.call-done = f32[32,432]{1,0:T(8,128)} async-done(((f32[256,432]{1,0:T(8,128)}), f32[32,432]{1,0:T(8,128)}) %reduce-scatter.9.cloned.1.call-update) | async-done | bytes 55312
  207.0 3.3 %collective-permute-start.3 = (bf16[1,18,256,130]{2,3,1,0:T(8,128)(2,1)}, bf16[1,18,256,130]{2,3,1,0:T(8,128)(2,1)S(1)}, u32[]{:S(2)}, u32[]{:S(2)}) collective-permute-start(bf16[1,18,256,130]{2,3,1,0:T(8,128)(2,1)} %pad.15.clone), channel_id=1, source_target_pairs={{0,16},{16,32},{32,48},{48,64},{64,80},{80,96},{96,112},{1,17},{17... | collective-permute-start | bytes 3594248 | tf_op jit(solution)/shard_map/ppermute | solution.py:12
  210.4 1.8 convolution_bitcast_fusion.10
  212.2 1.8 convolution_bitcast_fusion.9
  214.0 1.8 fusion.208
  215.8 68.7 %reduce-scatter.7.cloned.1.call-done = f32[32,432]{1,0:T(8,128)} async-done(((f32[256,432]{1,0:T(8,128)}), f32[32,432]{1,0:T(8,128)}) %reduce-scatter.7.cloned.1.call-update) | async-done | bytes 55312
  284.5 1.9 reshape.687
  286.4 2.0 copy.49
  288.3 1.7 broadcast_multiply_fusion.1
  (147 shorter events, 52.2 us)
Async XLA Ops:
  7.2 42.2 %all-gather.3.cloned.1.call-start = ((), (), s32[]{:S(2)}) async-start(), calls=%async_computation.2 | async-start | bytes 1114112 | tf_op jit(solution)/shard_map/all_gather | solution.py:34
  7.9 120.3 %all-gather.5.cloned.1.call-start = ((), (), s32[]{:S(2)}) async-start(), calls=%async_computation.3 | async-start | bytes 1114112 | tf_op jit(solution)/shard_map/all_gather | solution.py:34
  8.9 123.6 %collective-permute-start.4 = (bf16[1,18,16,130]{3,2,1,0:T(8,128)(2,1)S(1)}, bf16[1,18,16,130]{3,2,1,0:T(8,128)(2,1)S(1)}, u32[]{:S(2)}, u32[]{:S(2)}) collective-permute-start(bf16[1,18,16,130]{3,2,1,0:T(8,128)(2,1)S(1)} %pad.16), channel_id=1, source_target_pairs={{0,16},{16,32},{32,48},{48,64},{64,80},{80,96},{96,112},{1,17},{17... | collective-permute-start | bytes 224648 | tf_op jit(solution)/shard_map/ppermute | solution.py:12
  12.9 126.8 %collective-permute-start.5 = (bf16[1,18,16,130]{3,2,1,0:T(8,128)(2,1)S(1)}, bf16[1,18,16,130]{3,2,1,0:T(8,128)(2,1)S(1)}, u32[]{:S(2)}, u32[]{:S(2)}) collective-permute-start(bf16[1,18,16,130]{3,2,1,0:T(8,128)(2,1)S(1)} %pad.16), channel_id=1, source_target_pairs={{16,0},{32,16},{48,32},{64,48},{80,64},{96,80},{112,96},{17,1},{33... | collective-permute-start | bytes 224648 | tf_op jit(solution)/shard_map/ppermute | solution.py:15
  15.2 38.4 %collective-permute-start.6 = (bf16[1,18,16,130]{3,2,1,0:T(8,128)(2,1)S(1)}, bf16[1,18,16,130]{3,2,1,0:T(8,128)(2,1)S(1)}, u32[]{:S(2)}, u32[]{:S(2)}) collective-permute-start(bf16[1,18,16,130]{3,2,1,0:T(8,128)(2,1)S(1)} %pad.17), channel_id=1, source_target_pairs={{0,16},{16,32},{32,48},{48,64},{64,80},{80,96},{96,112},{1,17},{17... | collective-permute-start | bytes 224648 | tf_op jit(solution)/shard_map/ppermute | solution.py:12
  19.2 46.5 %collective-permute-start.7 = (bf16[1,18,16,130]{3,2,1,0:T(8,128)(2,1)S(1)}, bf16[1,18,16,130]{3,2,1,0:T(8,128)(2,1)S(1)}, u32[]{:S(2)}, u32[]{:S(2)}) collective-permute-start(bf16[1,18,16,130]{3,2,1,0:T(8,128)(2,1)S(1)} %pad.17), channel_id=1, source_target_pairs={{16,0},{32,16},{48,32},{64,48},{80,64},{96,80},{112,96},{17,1},{33... | collective-permute-start | bytes 224648 | tf_op jit(solution)/shard_map/ppermute | solution.py:15
  50.9 1.8 copy-start.1
  50.9 1.8 copy-start.6
  51.4 30.8 %collective-permute-start = (bf16[1,18,256,130]{2,3,1,0:T(8,128)(2,1)S(1)}, bf16[1,18,256,130]{2,3,1,0:T(8,128)(2,1)S(1)}, u32[]{:S(2)}, u32[]{:S(2)}) collective-permute-start(bf16[1,18,256,130]{2,3,1,0:T(8,128)(2,1)S(1)} %pad.14.clone), channel_id=1, source_target_pairs={{16,0},{32,16},{48,32},{64,48},{80,64},{96,80},{112,96},{17,1},{33... | collective-permute-start | bytes 3594248 | tf_op jit(solution)/shard_map/ppermute | solution.py:15
  53.6 31.7 %collective-permute-start.1 = (bf16[1,18,256,130]{2,3,1,0:T(8,128)(2,1)S(1)}, bf16[1,18,256,130]{2,3,1,0:T(8,128)(2,1)S(1)}, u32[]{:S(2)}, u32[]{:S(2)}) collective-permute-start(bf16[1,18,256,130]{2,3,1,0:T(8,128)(2,1)S(1)} %pad.14.clone), channel_id=1, source_target_pairs={{0,16},{16,32},{32,48},{48,64},{64,80},{80,96},{96,112},{1,17},{17... | collective-permute-start | bytes 3594248 | tf_op jit(solution)/shard_map/ppermute | solution.py:12
  62.0 0.9 copy-start.8
  91.3 113.7 %reduce-scatter.9.cloned.1.call-start = ((), (), s32[]{:S(2)}) async-start(), calls=%async_computation.5 | async-start | bytes 589824
  103.8 180.7 %reduce-scatter.7.cloned.1.call-start = ((), (), s32[]{:S(2)}) async-start(), calls=%async_computation.4 | async-start | bytes 589824
  129.6 2.9 copy-start
  131.2 158.8 %collective-permute-start.2 = (bf16[1,18,256,130]{2,3,1,0:T(8,128)(2,1)}, bf16[1,18,256,130]{2,3,1,0:T(8,128)(2,1)S(1)}, u32[]{:S(2)}, u32[]{:S(2)}) collective-permute-start(bf16[1,18,256,130]{2,3,1,0:T(8,128)(2,1)} %pad.15.clone), channel_id=1, source_target_pairs={{16,0},{32,16},{48,32},{64,48},{80,64},{96,80},{112,96},{17,1},{33... | collective-permute-start | bytes 3594248 | tf_op jit(solution)/shard_map/ppermute | solution.py:15
  135.3 0.9 copy-start.2
  207.0 86.8 %collective-permute-start.3 = (bf16[1,18,256,130]{2,3,1,0:T(8,128)(2,1)}, bf16[1,18,256,130]{2,3,1,0:T(8,128)(2,1)S(1)}, u32[]{:S(2)}, u32[]{:S(2)}) collective-permute-start(bf16[1,18,256,130]{2,3,1,0:T(8,128)(2,1)} %pad.15.clone), channel_id=1, source_target_pairs={{0,16},{16,32},{32,48},{48,64},{64,80},{80,96},{96,112},{1,17},{17... | collective-permute-start | bytes 3594248 | tf_op jit(solution)/shard_map/ppermute | solution.py:12
  288.3 2.7 copy-start.7
  296.6 0.9 copy-start.5
  299.1 0.9 copy-start.3
  299.1 1.0 copy-start.4
Sparse Core Ops, SparseCore 0:
  9.6 39.7 all-gather.2
  91.4 36.6 all-gather.4
  131.7 73.2 reduce-scatter.8
  208.9 75.5 reduce-scatter.6
where the time goes:
time: 310 us; the launch traced here: 308 us
  waiting for transfers between devices  191 us (62%)
  matrix products  48.3 us (16%)
  local copies, waits for them, and re-layouts  30.4 us (10%)
  starting transfers between devices  20.9 us (7%)
  between operations  14 us (5%)
  other arithmetic  3.27 us (1%)
    unnamed x6, waiting for transfers between devices  122 us
    all_gather x2, waiting for transfers between devices, cotangent_wide(): whole = lax.all_gather(field, 'chan', axis=2, tiled=True)  53.2 us
    unnamed x28, local copies, waits for them, and re-layouts  27.3 us
    dot_general x54, matrix products, layer_grads(): jnp.einsum('xzoy,io->xziy', back, weight[index], preferred_element_type=j...  27.1 us
    dot_general x54, matrix products, layer_grads(): lax.dot_general(window, grad_core, (((0, 1, 3), (0, 1, 3)), ((), ())), pr...  21.2 us
    ppermute x4, waiting for transfers between devices, extended(): lax.ppermute(lax.slice_in_dim(block, 0, width, axis=dim), axis, backward)  15.8 us
    ppermute x4, starting transfers between devices, extended(): lax.ppermute(lax.slice_in_dim(block, block.shape[dim] - width, None, axis...  15.4 us
  transfers between devices with their start and end apart: 12, of which 5 were waited for; matrix products, arithmetic and copies ran while one was open for 24% of the time, Pallas kernels for 0%

commit v1 on v0

v1 whole, which is shorter than its diff:
```python
import functools

import jax
import jax.numpy as jnp
from jax import lax
from jax.experimental import pallas as pl
from jax.experimental.pallas import tpu as pltpu
from jax.sharding import PartitionSpec as P

MESH = pl.DeviceIdType.MESH
OFFSETS = (-1, 0, 1)
CHIPS = ((2, 2), (2, 0), (1, 2), (3, 2), (1, 0), (3, 0), (0, 2))


def tap(a, b, c):
    return 9 * (a + 1) + 3 * (b + 1) + (c + 1)


def moved(value, step):
    if step == 0:
        return value
    width = value.shape[1]
    lane = lax.broadcasted_iota(jnp.int32, value.shape, 1)
    inside = lane < width - step if step > 0 else lane >= -step
    return jnp.where(inside, pltpu.roll(value, (-step) % width, 1), 0.0)


def kernel(
    dims,
    layer_hbm, pre_hbm, cot_hbm, w1_hbm, w2_hbm,
    out_ref, one_ref, two_ref,
    layer, pre, cot, w1, w2, hid, slope,
    got_cot, got_pre, cols_one, cols_two, prod, center,
    part, send_part, recv_part, send_q, recv_q,
    load_sem, gs, gr, fs, fr, hs, hr, qs, qr, ws, wr,
):
    ns, nz, own, ny, scale = dims
    groups = got_cot.shape[0] // own
    rows = own * nz
    wide = part.shape[0] // ns
    s = lax.axis_index("space")
    c = lax.axis_index("chan")
    zc, wc = lax.div(c, 4), lax.rem(c, 4)
    levels = groups // 4

    def chip(dz, dw):
        return lax.rem(zc + dz, levels) * 4 + (wc ^ dw)

    sibling = (s, c ^ 1)
    mine = pl.ds(pl.multiple_of(c * own, own), own)

    barrier = pltpu.get_barrier_semaphore()
    partners = [(s, chip(*d)) for d in CHIPS] + [(lax.rem(s + d, ns), c) for d in range(1, ns)] + [sibling]
    for p in partners:
        pl.semaphore_signal(barrier, inc=1, device_id=p, device_id_type=MESH)

    loads = [
        pltpu.make_async_copy(src, dst, load_sem.at[k])
        for k, (src, dst) in enumerate(
            ((cot_hbm.at[0], cot), (pre_hbm.at[0], pre), (layer_hbm.at[0], layer.at[1]), (w2_hbm, w2), (w1_hbm, w1))
        )
    ]
    for copy in loads:
        copy.start()

    loads[0].wait()
    for z in range(nz):
        got_cot[mine, z * ny:(z + 1) * ny] = cot[z]
    loads[1].wait()
    value = pre[...].astype(jnp.float32).reshape(rows, ny)
    sig = jax.nn.sigmoid(value)
    hid[1] = (value * sig).astype(jnp.bfloat16).reshape(nz, own, ny)
    slope[...] = sig * (1.0 + value * (1.0 - sig))
    loads[2].wait()

    def fill(cols, field, a):
        plane = field[a + 1].astype(jnp.float32).reshape(rows, ny)
        for b in OFFSETS:
            side = moved(plane, b).astype(jnp.bfloat16)
            for e in OFFSETS:
                k = tap(a, b, e)
                for z in range(nz):
                    if 0 <= z + e < nz:
                        piece = side[(z + e) * own:(z + e + 1) * own]
                    else:
                        piece = jnp.zeros((own, ny), jnp.bfloat16)
                    cols[k * own:(k + 1) * own, z * ny:(z + 1) * ny] = piece

    fill(cols_two, hid, 0)
    fill(cols_one, layer, 0)

    pl.semaphore_wait(barrier, len(partners))

    def start_gather(buf, row):
        home = pltpu.make_async_remote_copy(
            buf.at[mine], buf.at[mine], fs.at[row, 7], fr.at[row, 7], device_id=sibling, device_id_type=MESH
        )
        sends = []
        for k, d in enumerate(CHIPS):
            copy = pltpu.make_async_remote_copy(
                buf.at[mine], buf.at[mine], gs.at[row, k], gr.at[row, k], device_id=(s, chip(*d)), device_id_type=MESH
            )
            copy.start()
            sends.append(copy)
        home.start()
        return home, sends

    def forward_gather(buf, row, home, sends):
        passed = []
        for k in reversed(range(len(CHIPS))):
            dz, dw = CHIPS[k]
            sends[k].wait_recv()
            origin = pl.ds(pl.multiple_of(chip(levels - dz, dw) * own, own), own)
            copy = pltpu.make_async_remote_copy(
                buf.at[origin], buf.at[origin], fs.at[row, k], fr.at[row, k], device_id=sibling, device_id_type=MESH
            )
            copy.start()
            passed.append(copy)
        for copy in [home] + passed:
            copy.wait_recv()
        return [home] + passed + sends

    def halo(src, dst, sem, step, there):
        return pltpu.make_async_remote_copy(
            src, dst, hs.at[sem], hr.at[sem], device_id=(there, c), device_id_type=MESH
        )

    up, down = lax.rem(s + 1, ns), lax.rem(s + ns - 1, ns)

    halo_copies = [
        (halo(hid.at[1], hid.at[0], 0, 1, up), halo(hid.at[1], hid.at[2], 1, -1, down)),
        (halo(layer.at[1], layer.at[0], 2, 1, up), halo(layer.at[1], layer.at[2], 3, -1, down)),
    ]

    def start_pair(pair):
        @pl.when(s < ns - 1)
        def _():
            pair[0].start()

        @pl.when(s > 0)
        def _():
            pair[1].start()

    def finish_pair(pair, low, high):
        @pl.when(s > 0)
        def _():
            pair[0].wait_recv()

        @pl.when(s == 0)
        def _():
            low[...] = jnp.zeros(low.shape, low.dtype)

        @pl.when(s < ns - 1)
        def _():
            pair[1].wait_recv()

        @pl.when(s == ns - 1)
        def _():
            high[...] = jnp.zeros(high.shape, high.dtype)

    def sent_pair(pair):
        @pl.when(s < ns - 1)
        def _():
            pair[0].wait_send()

        @pl.when(s > 0)
        def _():
            pair[1].wait_send()

    def plane_sum(weight, got, a):
        lo = tap(a, -1, -1) * own
        left = weight[9 * (a + 1):9 * (a + 2)].reshape(9 * own, groups * own)
        prod[lo:lo + 9 * own, :] = jnp.dot(left, got[...], preferred_element_type=jnp.float32)
        result = []
        for z in range(nz):
            total = None
            for b in OFFSETS:
                column = None
                for e in OFFSETS:
                    if 0 <= z - e < nz:
                        k = tap(a, b, e)
                        term = prod[k * own:(k + 1) * own, (z - e) * ny:(z - e + 1) * ny]
                        column = term if column is None else column + term
                column = moved(column, -b)
                total = column if total is None else total + column
            result.append(total)
        return result

    def q_pair(row):
        def copy(slot, there):
            return pltpu.make_async_remote_copy(
                send_q.at[row, slot], recv_q.at[row, slot], qs.at[row, slot], qr.at[row, slot],
                device_id=(there, c), device_id_type=MESH,
            )

        return copy(0, up), copy(1, down)

    def input_side(weight, got, row):
        pair = q_pair(row)
        for slot, a in ((0, 1), (1, -1)):
            for z, value in enumerate(plane_sum(weight, got, a)):
                send_q[row, slot, z] = value.astype(jnp.bfloat16)
        start_pair(pair)
        for z, value in enumerate(plane_sum(weight, got, 0)):
            center[z * own:(z + 1) * own, :] = value
        return pair

    def input_total(pair, row):
        finish_pair(pair, recv_q.at[row, 0], recv_q.at[row, 1])
        low = recv_q[row, 0].astype(jnp.float32).reshape(rows, ny)
        high = recv_q[row, 1].astype(jnp.float32).reshape(rows, ny)
        return center[...] + low + high

    def weight_side(cols, got, row):
        part[...] = lax.dot_general(
            got[...], cols[...], (((1,), (1,)), ((), ())), preferred_element_type=jnp.float32
        )
        send_part[row] = part[...].astype(jnp.bfloat16)
        copies = []
        for d in range(1, ns):
            there = lax.rem(s + d, ns)
            block = pl.ds(pl.multiple_of(there * wide, wide), wide)
            copy = pltpu.make_async_remote_copy(
                send_part.at[row, block], recv_part.at[row, d - 1], ws.at[row, d - 1], wr.at[row, d - 1],
                device_id=(there, c), device_id_type=MESH,
            )
            copy.start()
            copies.append(copy)
        return part[pl.ds(pl.multiple_of(s * wide, wide), wide), :], copies

    def weight_total(total, copies, row, ref):
        for d, copy in enumerate(copies):
            copy.wait_recv()
            total = total + recv_part[row, d].astype(jnp.float32)
        ref[...] = (total * scale).T.reshape(ref.shape)

    home, sends = start_gather(got_cot, 0)
    start_pair(halo_copies[0])
    start_pair(halo_copies[1])
    loads[3].wait()
    loads[4].wait()
    pending = forward_gather(got_cot, 0, home, sends)
    pair_two = input_side(w2, got_cot, 0)
    finish_pair(halo_copies[0], hid.at[0], hid.at[2])
    fill(cols_two, hid, -1)
    fill(cols_two, hid, 1)
    total_two, copies_two = weight_side(cols_two, got_cot, 0)

    grad = (input_total(pair_two, 0) * slope[...]).astype(jnp.bfloat16)
    for z in range(nz):
        got_pre[mine, z * ny:(z + 1) * ny] = grad[z * own:(z + 1) * own]
    home, sends = start_gather(got_pre, 1)
    finish_pair(halo_copies[1], layer.at[0], layer.at[2])
    fill(cols_one, layer, -1)
    fill(cols_one, layer, 1)
    weight_total(total_two, copies_two, 0, two_ref)
    pending += forward_gather(got_pre, 1, home, sends)

    total_one, copies_one = weight_side(cols_one, got_pre, 1)
    pair_one = input_side(w1, got_pre, 1)
    out_ref[0] = input_total(pair_one, 1).astype(jnp.bfloat16).reshape(nz, own, ny)
    weight_total(total_one, copies_one, 1, one_ref)

    for copy in pending + copies_two + copies_one:
        copy.wait_send()
    for pair in halo_copies + [pair_two, pair_one]:
        sent_pair(pair)


def solution(mesh):
    ns, groups = mesh.shape["space"], mesh.shape["chan"]

    def shards(layer_input, pre_act, out_grad, weight_one, weight_two):
        _, nz, own, ny = layer_input.shape
        taps, _, chans = weight_one.shape
        scale = float(ns * ny * nz) ** -0.5
        any_space = pl.BlockSpec(memory_space=pl.ANY)
        vmem = pl.BlockSpec(memory_space=pltpu.VMEM)
        bf, f32 = jnp.bfloat16, jnp.float32
        dma = pltpu.SemaphoreType.DMA
        return pl.pallas_call(
            functools.partial(kernel, (ns, nz, own, ny, scale)),
            out_shape=(
                jax.ShapeDtypeStruct(layer_input.shape, bf),
                jax.ShapeDtypeStruct((taps, own, chans // ns), f32),
                jax.ShapeDtypeStruct((taps, own, chans // ns), f32),
            ),
            in_specs=[any_space] * 5,
            out_specs=(vmem, vmem, vmem),
            scratch_shapes=[
                pltpu.VMEM((3, nz, own, ny), bf),
                pltpu.VMEM((nz, own, ny), bf),
                pltpu.VMEM((nz, own, ny), bf),
                pltpu.VMEM(weight_one.shape, bf),
                pltpu.VMEM(weight_two.shape, bf),
                pltpu.VMEM((3, nz, own, ny), bf),
                pltpu.VMEM((nz * own, ny), f32),
                pltpu.VMEM((chans, nz * ny), bf),
                pltpu.VMEM((chans, nz * ny), bf),
                pltpu.VMEM((taps * own, nz * ny), bf),
                pltpu.VMEM((taps * own, nz * ny), bf),
                pltpu.VMEM((taps * own, nz * ny), f32),
                pltpu.VMEM((nz * own, ny), f32),
                pltpu.VMEM((chans, taps * own), f32),
                pltpu.VMEM((2, chans, taps * own), bf),
                pltpu.VMEM((2, ns - 1, chans // ns, taps * own), bf),
                pltpu.VMEM((2, 2, nz, own, ny), bf),
                pltpu.VMEM((2, 2, nz, own, ny), bf),
                dma((5,)),
                dma((2, 7)),
                dma((2, 7)),
                dma((2, 8)),
                dma((2, 8)),
                dma((4,)),
                dma((4,)),
                dma((2, 2)),
                dma((2, 2)),
                dma((2, 7)),
                dma((2, 7)),
            ],
            compiler_params=pltpu.CompilerParams(
                collective_id=0, has_side_effects=True, vmem_limit_bytes=48 * 1024 * 1024
            ),
        )(layer_input, pre_act, out_grad, weight_one, weight_two)

    wide, narrow = P("space", None, "chan", None), P(None, "chan", None)
    return jax.shard_map(
        shards,
        mesh=mesh,
        in_specs=(wide, wide, wide, narrow, narrow),
        out_specs=(wide, P(None, "chan", "space"), P(None, "chan", "space")),
        check_vma=False,
    )
```

time: 310 us -> 48.2 us (0.16)
  waiting for transfers between devices: 191 us -> 0 us
  matrix products: 48.3 us -> 0 us
  Pallas kernels: 0 us -> 40.9 us
  local copies, waits for them, and re-layouts: 30.4 us -> 6.38 us
  starting transfers between devices: 20.9 us -> 0 us
  between operations: 14 us -> 0.65 us
  other arithmetic: 3.27 us -> 0 us
    unnamed x6 -> x0, waiting for transfers between devices: 122 us -> none
    all_gather x2 -> x0, waiting for transfers between devices: 53.2 us -> none  [cotangent_wide(): whole = lax.all_gather(field, 'chan', axis=2, tiled=True)]
    dot_general x108 -> x0, matrix products: 48.3 us -> none  [the longest x54 27.1 us: layer_grads(): jnp.einsum('xzoy,io->xziy', back, weight[index], preferred_element_type=j...]
    pallas_call x0 -> x1, Pallas kernels: none -> 40.9 us  [shards(): pl.pallas_call(functools.partial(kernel, (ns, nz, own, ny, scale)), out_s...]
    unnamed x28 -> x13, local copies, waits for them, and re-layouts: 27.3 us -> 6.38 us
    ppermute x8 -> x0, starting transfers between devices: 20.5 us -> none  [the longest x4 15.4 us: extended(): lax.ppermute(lax.slice_in_dim(block, block.shape[dim] - width, None, axis...]
    ppermute x8 -> x0, waiting for transfers between devices: 15.8 us -> none  [the longest x4 15.8 us: extended(): lax.ppermute(lax.slice_in_dim(block, 0, width, axis=dim), axis, backward)]
  transfers between devices with their start and end apart: 12 -> 0, of which waited for: 5 -> 0; matrix products, arithmetic and copies ran while one was open for 24% -> 0% of each run, Pallas kernels for 0% -> 0%
where the time goes in v1:
time: 48.2 us; the launch traced here: 47.9 us
  Pallas kernels  40.9 us (85%)
  local copies, waits for them, and re-layouts  6.38 us (13%)
  between operations  0.65 us (1%)
    pallas_call x1, Pallas kernels, shards(): pl.pallas_call(functools.partial(kernel, (ns, nz, own, ny, scale)), out_s...  40.9 us
    unnamed x13, local copies, waits for them, and re-layouts  6.38 us

profile of v1, /device:TPU:1, one launch (start us, length us, event | category | flops | bytes accessed | tf_op | source)
XLA Modules:
  0.0 47.9 jit_solution(867890824904780827)
XLA Ops:
  0.6 0.0 copy-start
  0.6 0.9 %copy-done = bf16[27,16,256]{2,1,0:T(8,128)(2,1)S(1)} copy-done((bf16[27,16,256]{2,1,0:T(8,128)(2,1)S(1)}, bf16[27,16,256]{2,1,0:T(8,128)(2,1)}, u32[]{:S(2)}) %copy-start) | copy-done | bytes 221208
  1.6 0.0 copy-start.1
  1.6 0.9 %copy-done.1 = bf16[27,16,256]{2,1,0:T(8,128)(2,1)S(1)} copy-done((bf16[27,16,256]{2,1,0:T(8,128)(2,1)S(1)}, bf16[27,16,256]{2,1,0:T(8,128)(2,1)}, u32[]{:S(2)}) %copy-start.1) | copy-done | bytes 221208
  2.5 0.0 copy-start.2
  2.5 0.8 %copy-done.2 = bf16[1,16,16,128]{3,2,1,0:T(8,128)(2,1)S(1)} copy-done((bf16[1,16,16,128]{3,2,1,0:T(8,128)(2,1)S(1)}, bf16[1,16,16,128]{3,2,1,0:T(8,128)(2,1)}, u32[]{:S(2)}) %copy-start.2) | copy-done | bytes 65560
  3.3 0.0 copy-start.3
  3.3 0.8 %copy-done.3 = bf16[1,16,16,128]{3,2,1,0:T(8,128)(2,1)S(1)} copy-done((bf16[1,16,16,128]{3,2,1,0:T(8,128)(2,1)S(1)}, bf16[1,16,16,128]{3,2,1,0:T(8,128)(2,1)}, u32[]{:S(2)}) %copy-start.3) | copy-done | bytes 65560
  4.2 0.0 copy-start.4
  4.2 0.8 %copy-done.4 = bf16[1,16,16,128]{3,2,1,0:T(8,128)(2,1)S(1)} copy-done((bf16[1,16,16,128]{3,2,1,0:T(8,128)(2,1)S(1)}, bf16[1,16,16,128]{3,2,1,0:T(8,128)(2,1)}, u32[]{:S(2)}) %copy-start.4) | copy-done | bytes 65560
  5.0 40.9 %shard_map.76 = (bf16[1,16,16,128]{3,2,1,0:T(8,128)(2,1)S(1)}, f32[27,16,32]{2,1,0:T(8,128)S(1)}, f32[27,16,32]{2,1,0:T(8,128)S(1)}) custom-call(bf16[1,16,16,128]{3,2,1,0:T(8,128)(2,1)S(1)} %copy-done.2, bf16[1,16,16,128]{3,2,1,0:T(8,128)(2,1)S(1)} %copy-done.3, bf16[1,16,16,128]{3,2,1,0:T(8,128)(2,1)S(1)} %copy-done.4, bf16[27,16,256]{2,1,0:T(8,128)(2,1)S(1)} %copy-done, ...), custom_call_target="tpu_custom_call" | custom-call | tf_op jit(solution)/shard_map/pallas_call | solution.py:281
  45.9 0.6 %copy.11 = bf16[1,16,16,128]{3,2,1,0:T(8,128)(2,1)} copy(bf16[1,16,16,128]{3,2,1,0:T(8,128)(2,1)S(1)} %get-tuple-element.6) | data formatting | bytes 131072
  46.5 0.7 %copy.12 = f32[27,16,32]{2,1,0:T(8,128)} copy(f32[27,16,32]{2,1,0:T(8,128)S(1)} %get-tuple-element.7) | data formatting | bytes 110592
  47.2 0.7 %copy.13 = f32[27,16,32]{2,1,0:T(8,128)} copy(f32[27,16,32]{2,1,0:T(8,128)S(1)} %get-tuple-element.8) | data formatting | bytes 110592
Async XLA Ops:
  0.6 0.9 %copy-start = (bf16[27,16,256]{2,1,0:T(8,128)(2,1)S(1)}, bf16[27,16,256]{2,1,0:T(8,128)(2,1)}, u32[]{:S(2)}) copy-start(bf16[27,16,256]{2,1,0:T(8,128)(2,1)} %w1_hbm.1) | copy-start | bytes 663556
  1.6 0.9 %copy-start.1 = (bf16[27,16,256]{2,1,0:T(8,128)(2,1)S(1)}, bf16[27,16,256]{2,1,0:T(8,128)(2,1)}, u32[]{:S(2)}) copy-start(bf16[27,16,256]{2,1,0:T(8,128)(2,1)} %w2_hbm.1) | copy-start | bytes 663556
  2.5 0.8 %copy-start.2 = (bf16[1,16,16,128]{3,2,1,0:T(8,128)(2,1)S(1)}, bf16[1,16,16,128]{3,2,1,0:T(8,128)(2,1)}, u32[]{:S(2)}) copy-start(bf16[1,16,16,128]{3,2,1,0:T(8,128)(2,1)} %layer_hbm.1) | copy-start | bytes 196612
  3.3 0.8 %copy-start.3 = (bf16[1,16,16,128]{3,2,1,0:T(8,128)(2,1)S(1)}, bf16[1,16,16,128]{3,2,1,0:T(8,128)(2,1)}, u32[]{:S(2)}) copy-start(bf16[1,16,16,128]{3,2,1,0:T(8,128)(2,1)} %pre_hbm.1) | copy-start | bytes 196612
  4.2 0.8 %copy-start.4 = (bf16[1,16,16,128]{3,2,1,0:T(8,128)(2,1)S(1)}, bf16[1,16,16,128]{3,2,1,0:T(8,128)(2,1)}, u32[]{:S(2)}) copy-start(bf16[1,16,16,128]{3,2,1,0:T(8,128)(2,1)} %cot_hbm.1) | copy-start | bytes 196612

commit v2 on v1

--- a/solution.py
+++ b/solution.py
@@ -267,6 +267,17 @@
         sent_pair(pair)
 
 
+def hand_out(one_ref, two_ref, three_ref, one_out, two_out, three_out, sem):
+    copies = [
+        pltpu.make_async_copy(src, dst, sem.at[k])
+        for k, (src, dst) in enumerate(((one_ref, one_out), (two_ref, two_out), (three_ref, three_out)))
+    ]
+    for copy in copies:
+        copy.start()
+    for copy in copies:
+        copy.wait()
+
+
 def solution(mesh):
     ns, groups = mesh.shape["space"], mesh.shape["chan"]
 
@@ -278,7 +289,7 @@
         vmem = pl.BlockSpec(memory_space=pltpu.VMEM)
         bf, f32 = jnp.bfloat16, jnp.float32
         dma = pltpu.SemaphoreType.DMA
-        return pl.pallas_call(
+        results = pl.pallas_call(
             functools.partial(kernel, (ns, nz, own, ny, scale)),
             out_shape=(
                 jax.ShapeDtypeStruct(layer_input.shape, bf),
@@ -321,7 +332,15 @@
             compiler_params=pltpu.CompilerParams(
                 collective_id=0, has_side_effects=True, vmem_limit_bytes=48 * 1024 * 1024
             ),
-        )(layer_input, pre_act, out_grad, weight_one, weight_two)
+        )(*[pltpu.with_memory_space_constraint(v, pltpu.HBM) for v in (layer_input, pre_act, out_grad, weight_one, weight_two)])
+        return pl.pallas_call(
+            hand_out,
+            out_shape=tuple(jax.ShapeDtypeStruct(v.shape, v.dtype) for v in results),
+            in_specs=[vmem] * 3,
+            out_specs=(any_space,) * 3,
+            scratch_shapes=[dma((3,))],
+            compiler_params=pltpu.CompilerParams(vmem_limit_bytes=1024 * 1024),
+        )(*results)
 
     wide, narrow = P("space", None, "chan", None), P(None, "chan", None)
     return jax.shard_map(

time: 48.2 us -> 42.5 us (0.88)
  local copies, waits for them, and re-layouts: 6.38 us -> 0 us
  Pallas kernels: 40.9 us -> 41.8 us
    unnamed x13 -> x0, local copies, waits for them, and re-layouts: 6.38 us -> none
    pallas_call x0 -> x1, Pallas kernels: none -> 0.81 us  [shards(): pl.pallas_call(hand_out, out_shape=tuple((jax.ShapeDtypeStruct(v.shape, v...]
where the time goes in v2:
time: 42.5 us; the launch traced here: 42.4 us
  Pallas kernels  41.8 us (98%)
  between operations  0.64 us (2%)
    pallas_call x1, Pallas kernels, shards(): pl.pallas_call(functools.partial(kernel, (ns, nz, own, ny, scale)), out_s...  41 us

profile of v2, /device:TPU:1, one launch (start us, length us, event | category | flops | bytes accessed | tf_op | source)
XLA Modules:
  0.0 42.4 jit_solution(460723329284199417)
XLA Ops:
  0.6 41.0 %shard_map.76 = (bf16[1,16,16,128]{3,2,1,0:T(8,128)(2,1)S(1)}, f32[27,16,32]{2,1,0:T(8,128)S(1)}, f32[27,16,32]{2,1,0:T(8,128)S(1)}) custom-call(bf16[1,16,16,128]{3,2,1,0:T(8,128)(2,1)} %layer_hbm.1, bf16[1,16,16,128]{3,2,1,0:T(8,128)(2,1)} %pre_hbm.1, bf16[1,16,16,128]{3,2,1,0:T(8,128)(2,1)} %cot_hbm.1, bf16[27,16,256]{2,1,0:T(8,128)(2,1)} %w1_hbm.1, ...), custom_call_target="tpu_custom_call" | custom-call | tf_op jit(solution)/shard_map/pallas_call | solution.py:292
  41.6 0.8 %shard_map.77 = (bf16[1,16,16,128]{3,2,1,0:T(8,128)(2,1)}, f32[27,16,32]{2,1,0:T(8,128)}, f32[27,16,32]{2,1,0:T(8,128)}) custom-call(bf16[1,16,16,128]{3,2,1,0:T(8,128)(2,1)S(1)} %get-tuple-element.6.one_ref, f32[27,16,32]{2,1,0:T(8,128)S(1)} %get-tuple-element.7.two_ref, f32[27,16,32]{2,1,0:T(8,128)S(1)} %get-tuple-element.8.three_ref), custom_call_target="tpu_custom_call" | custom-call | tf_op jit(solution)/shard_map/pallas_call | solution.py:336

commit v3 on v2

v3 whole, which is shorter than its diff:
```python
import functools

import jax
import jax.numpy as jnp
from jax import lax
from jax.experimental import pallas as pl
from jax.experimental.pallas import tpu as pltpu
from jax.sharding import PartitionSpec as P

MESH = pl.DeviceIdType.MESH
OFFSETS = (-1, 0, 1)
CHIPS = ((2, 2), (2, 0), (1, 2), (3, 2), (1, 0), (3, 0), (0, 2))


def tap(a, b, c):
    return 9 * (a + 1) + 3 * (b + 1) + (c + 1)


def moved(value, step):
    if step == 0:
        return value
    width = value.shape[1]
    lane = lax.broadcasted_iota(jnp.int32, value.shape, 1)
    inside = lane < width - step if step > 0 else lane >= -step
    return jnp.where(inside, pltpu.roll(value, (-step) % width, 1), 0.0)


def kernel(
    dims,
    layer_hbm, pre_hbm, cot_hbm, w1_hbm, w2_hbm,
    out_ref, one_ref, two_ref,
    layer, pre, cot, w1, w2, hid, slope,
    got_cot, got_pre, cols_one, cols_two, prod, center,
    part, send_part, recv_part, send_q, recv_q,
    load_sem, gs, gr, fs, fr, hs, hr, qs, qr, ws, wr,
):
    ns, nz, own, ny, scale, (ends_one, ends_two, ends_three) = dims
    groups = got_cot.shape[0] // own
    rows = own * nz
    wide = part.shape[0] // ns
    s = lax.axis_index("space")
    c = lax.axis_index("chan")
    zc, wc = lax.div(c, 4), lax.rem(c, 4)
    levels = groups // 4

    def chip(dz, dw):
        return lax.rem(zc + dz, levels) * 4 + (wc ^ dw)

    sibling = (s, c ^ 1)
    mine = pl.ds(pl.multiple_of(c * own, own), own)

    barrier = pltpu.get_barrier_semaphore()
    partners = [(s, chip(*d)) for d in CHIPS] + [(lax.rem(s + d, ns), c) for d in range(1, ns)] + [sibling]
    for p in partners:
        pl.semaphore_signal(barrier, inc=1, device_id=p, device_id_type=MESH)

    loads = [
        pltpu.make_async_copy(src, dst, load_sem.at[k])
        for k, (src, dst) in enumerate(
            ((cot_hbm.at[0], cot), (pre_hbm.at[0], pre), (layer_hbm.at[0], layer.at[1]), (w2_hbm, w2), (w1_hbm, w1))
        )
    ]
    for copy in loads:
        copy.start()

    loads[0].wait()
    for z in range(nz):
        got_cot[mine, z * ny:(z + 1) * ny] = cot[z]
    pl.semaphore_wait(barrier, len(partners))

    def lanes(j, ends):
        start = ends[j - 1] if j else 0
        return pl.ds(start * ny, (ends[j] - start) * ny)

    def start_gather(buf, row, j, ends):
        span = lanes(j, ends)
        sends = []
        for k, d in enumerate(CHIPS):
            copy = pltpu.make_async_remote_copy(
                buf.at[mine, span], buf.at[mine, span], gs.at[row, j, k], gr.at[row, j, k],
                device_id=(s, chip(*d)), device_id_type=MESH,
            )
            copy.start()
            sends.append(copy)
        home = pltpu.make_async_remote_copy(
            buf.at[mine, span], buf.at[mine, span], fs.at[row, j, len(CHIPS)], fr.at[row, j, len(CHIPS)],
            device_id=sibling, device_id_type=MESH,
        )
        home.start()
        return home, sends

    def forward_gather(buf, row, j, ends, home, sends):
        span = lanes(j, ends)
        passed = []
        for k in reversed(range(len(CHIPS))):
            dz, dw = CHIPS[k]
            sends[k].wait_recv()
            origin = pl.ds(pl.multiple_of(chip(levels - dz, dw) * own, own), own)
            copy = pltpu.make_async_remote_copy(
                buf.at[origin, span], buf.at[origin, span], fs.at[row, j, k], fr.at[row, j, k],
                device_id=sibling, device_id_type=MESH,
            )
            copy.start()
            passed.append(copy)
        for copy in [home] + passed:
            copy.wait_recv()
        return [home] + passed + sends

    def halo(src, dst, sem, there):
        return pltpu.make_async_remote_copy(
            src, dst, hs.at[sem], hr.at[sem], device_id=(there, c), device_id_type=MESH
        )

    up, down = lax.rem(s + 1, ns), lax.rem(s + ns - 1, ns)

    def start_pair(pair):
        @pl.when(s < ns - 1)
        def _():
            pair[0].start()

        @pl.when(s > 0)
        def _():
            pair[1].start()

    def finish_pair(pair, low, high):
        @pl.when(s > 0)
        def _():
            pair[0].wait_recv()

        @pl.when(s == 0)
        def _():
            low[...] = jnp.zeros(low.shape, low.dtype)

        @pl.when(s < ns - 1)
        def _():
            pair[1].wait_recv()

        @pl.when(s == ns - 1)
        def _():
            high[...] = jnp.zeros(high.shape, high.dtype)

    def sent_pair(pair):
        @pl.when(s < ns - 1)
        def _():
            pair[0].wait_send()

        @pl.when(s > 0)
        def _():
            pair[1].wait_send()

    def fill(cols, field, a):
        plane = field[a + 1].astype(jnp.float32).reshape(rows, ny)
        for b in OFFSETS:
            side = moved(plane, b).astype(jnp.bfloat16)
            for e in OFFSETS:
                k = tap(a, b, e)
                for z in range(nz):
                    if 0 <= z + e < nz:
                        piece = side[(z + e) * own:(z + e + 1) * own]
                    else:
                        piece = jnp.zeros((own, ny), jnp.bfloat16)
                    cols[k * own:(k + 1) * own, z * ny:(z + 1) * ny] = piece

    def plane_sum(a, first, last):
        for z in range(first, last):
            total = None
            for b in OFFSETS:
                column = None
                for e in OFFSETS:
                    if 0 <= z - e < nz:
                        k = tap(a, b, e)
                        term = prod[k * own:(k + 1) * own, (z - e) * ny:(z - e + 1) * ny]
                        column = term if column is None else column + term
                column = moved(column, -b)
                total = column if total is None else total + column
            yield z, total

    def input_side(weight, got, row, j, ends_in, ends_out):
        span = lanes(j, ends_in)
        first, last = (ends_out[j - 1] if j else 0), ends_out[j]
        field = got[:, span]

        def product(a):
            lo = tap(a, -1, -1) * own
            left = weight[9 * (a + 1):9 * (a + 2)].reshape(9 * own, groups * own)
            prod[lo:lo + 9 * own, span] = jnp.dot(left, field, preferred_element_type=jnp.float32)

        def copy(slot, there):
            part_z = pl.ds(first, last - first)
            return pltpu.make_async_remote_copy(
                send_q.at[row, slot, part_z], recv_q.at[row, slot, part_z], qs.at[row, j, slot], qr.at[row, j, slot],
                device_id=(there, c), device_id_type=MESH,
            )

        pair = copy(0, up), copy(1, down)
        for slot, a in ((0, 1), (1, -1)):
            product(a)
            for z, value in plane_sum(a, first, last):
                send_q[row, slot, z] = value.astype(jnp.bfloat16)
        start_pair(pair)
        product(0)
        for z, value in plane_sum(0, first, last):
            center[z * own:(z + 1) * own, :] = value
        return pair

    def input_total(pair, row, j, ends):
        first, last = (ends[j - 1] if j else 0), ends[j]
        part_z = pl.ds(first, last - first)
        finish_pair(pair, recv_q.at[row, 0, part_z], recv_q.at[row, 1, part_z])
        low = recv_q[row, 0, first:last].astype(jnp.float32).reshape((last - first) * own, ny)
        high = recv_q[row, 1, first:last].astype(jnp.float32).reshape((last - first) * own, ny)
        return first, last, center[first * own:last * own, :] + low + high

    def weight_product(cols, got, span):
        return lax.dot_general(
            got[:, span], cols[:, span], (((1,), (1,)), ((), ())), preferred_element_type=jnp.float32
        )

    def weight_pack(row):
        send_part[row] = part[...].astype(jnp.bfloat16)
        return part[pl.ds(pl.multiple_of(s * wide, wide), wide), :]

    def weight_send(row):
        copies = []
        for d in range(1, ns):
            there = lax.rem(s + d, ns)
            block = pl.ds(pl.multiple_of(there * wide, wide), wide)
            copy = pltpu.make_async_remote_copy(
                send_part.at[row, block], recv_part.at[row, d - 1], ws.at[row, d - 1], wr.at[row, d - 1],
                device_id=(there, c), device_id_type=MESH,
            )
            copy.start()
            copies.append(copy)
        return copies

    def weight_total(total, copies, row, ref):
        for d, copy in enumerate(copies):
            copy.wait_recv()
            total = total + recv_part[row, d].astype(jnp.float32)
        ref[...] = (total * scale).T.reshape(ref.shape)

    chunks = len(ends_one)
    started = [start_gather(got_cot, 0, j, ends_one) for j in range(chunks)]

    loads[1].wait()
    value = pre[...].astype(jnp.float32).reshape(rows, ny)
    sig = jax.nn.sigmoid(value)
    hid[1] = (value * sig).astype(jnp.bfloat16).reshape(nz, own, ny)
    slope[...] = sig * (1.0 + value * (1.0 - sig))
    loads[2].wait()
    halo_copies = [
        (halo(hid.at[1], hid.at[0], 0, up), halo(hid.at[1], hid.at[2], 1, down)),
        (halo(layer.at[1], layer.at[0], 2, up), halo(layer.at[1], layer.at[2], 3, down)),
    ]
    start_pair(halo_copies[0])
    start_pair(halo_copies[1])
    fill(cols_two, hid, 0)
    fill(cols_one, layer, 0)
    loads[3].wait()
    loads[4].wait()

    pending, pairs = [], []
    for j in range(chunks):
        pending += forward_gather(got_cot, 0, j, ends_one, *started[j])
        pairs.append(input_side(w2, got_cot, 0, j, ends_one, ends_two))
    started = []
    for j in range(chunks):
        first, last, grad = input_total(pairs[j], 0, j, ends_two)
        grad = (grad * slope[first * own:last * own, :]).astype(jnp.bfloat16)
        for z in range(first, last):
            got_pre[mine, z * ny:(z + 1) * ny] = grad[(z - first) * own:(z - first + 1) * own]
        started.append(start_gather(got_pre, 1, j, ends_two))
    finish_pair(halo_copies[0], hid.at[0], hid.at[2])
    fill(cols_two, hid, -1)
    fill(cols_two, hid, 1)
    part[...] = weight_product(cols_two, got_cot, pl.ds(0, nz * ny))
    total_two = weight_pack(0)

    finish_pair(halo_copies[1], layer.at[0], layer.at[2])
    fill(cols_one, layer, -1)
    fill(cols_one, layer, 1)

    for j in range(chunks):
        pending += forward_gather(got_pre, 1, j, ends_two, *started[j])
        if j == 0:
            copies_two = weight_send(0)
        piece = weight_product(cols_one, got_pre, lanes(j, ends_two))
        part[...] = piece if j == 0 else part[...] + piece
        if j == chunks - 1:
            total_one = weight_pack(1)
            copies_one = weight_send(1)
        pairs.append(input_side(w1, got_pre, 1, j, ends_two, ends_three))
    weight_total(total_two, copies_two, 0, two_ref)
    for j in range(chunks):
        first, last, grad = input_total(pairs[chunks + j], 1, j, ends_three)
        out_ref[0, first:last] = grad.astype(jnp.bfloat16).reshape(last - first, own, ny)
    weight_total(total_one, copies_one, 1, one_ref)

    for copy in pending + copies_two + copies_one:
        copy.wait_send()
    for pair in halo_copies + pairs:
        sent_pair(pair)


def hand_out(one_ref, two_ref, three_ref, one_out, two_out, three_out, sem):
    copies = [
        pltpu.make_async_copy(src, dst, sem.at[k])
        for k, (src, dst) in enumerate(((one_ref, one_out), (two_ref, two_out), (three_ref, three_out)))
    ]
    for copy in copies:
        copy.start()
    for copy in copies:
        copy.wait()


def solution(mesh):
    ns, groups = mesh.shape["space"], mesh.shape["chan"]

    def shards(layer_input, pre_act, out_grad, weight_one, weight_two):
        _, nz, own, ny = layer_input.shape
        taps, _, chans = weight_one.shape
        scale = float(ns * ny * nz) ** -0.5
        chunks = 2
        ends = tuple(
            tuple(nz if j == chunks - 1 else nz * (j + 1) // chunks + shift for j in range(chunks)) for shift in (1, 0, -1)
        )
        any_space = pl.BlockSpec(memory_space=pl.ANY)
        vmem = pl.BlockSpec(memory_space=pltpu.VMEM)
        bf, f32 = jnp.bfloat16, jnp.float32
        dma = pltpu.SemaphoreType.DMA
        results = pl.pallas_call(
            functools.partial(kernel, (ns, nz, own, ny, scale, ends)),
            out_shape=(
                jax.ShapeDtypeStruct(layer_input.shape, bf),
                jax.ShapeDtypeStruct((taps, own, chans // ns), f32),
                jax.ShapeDtypeStruct((taps, own, chans // ns), f32),
            ),
            in_specs=[any_space] * 5,
            out_specs=(vmem, vmem, vmem),
            scratch_shapes=[
                pltpu.VMEM((3, nz, own, ny), bf),
                pltpu.VMEM((nz, own, ny), bf),
                pltpu.VMEM((nz, own, ny), bf),
                pltpu.VMEM(weight_one.shape, bf),
                pltpu.VMEM(weight_two.shape, bf),
                pltpu.VMEM((3, nz, own, ny), bf),
                pltpu.VMEM((nz * own, ny), f32),
                pltpu.VMEM((chans, nz * ny), bf),
                pltpu.VMEM((chans, nz * ny), bf),
                pltpu.VMEM((taps * own, nz * ny), bf),
                pltpu.VMEM((taps * own, nz * ny), bf),
                pltpu.VMEM((taps * own, nz * ny), f32),
                pltpu.VMEM((nz * own, ny), f32),
                pltpu.VMEM((chans, taps * own), f32),
                pltpu.VMEM((2, chans, taps * own), bf),
                pltpu.VMEM((2, ns - 1, chans // ns, taps * own), bf),
                pltpu.VMEM((2, 2, nz, own, ny), bf),
                pltpu.VMEM((2, 2, nz, own, ny), bf),
                dma((5,)),
                dma((2, chunks, len(CHIPS))),
                dma((2, chunks, len(CHIPS))),
                dma((2, chunks, len(CHIPS) + 1)),
                dma((2, chunks, len(CHIPS) + 1)),
                dma((4,)),
                dma((4,)),
                dma((2, chunks, 2)),
                dma((2, chunks, 2)),
                dma((2, ns - 1)),
                dma((2, ns - 1)),
            ],
            compiler_params=pltpu.CompilerParams(
                collective_id=0, has_side_effects=True, vmem_limit_bytes=48 * 1024 * 1024
            ),
        )(*[pltpu.with_memory_space_constraint(v, pltpu.HBM) for v in (layer_input, pre_act, out_grad, weight_one, weight_two)])
        return pl.pallas_call(
            hand_out,
            out_shape=tuple(jax.ShapeDtypeStruct(v.shape, v.dtype) for v in results),
            in_specs=[vmem] * 3,
            out_specs=(any_space,) * 3,
            scratch_shapes=[dma((3,))],
            compiler_params=pltpu.CompilerParams(vmem_limit_bytes=1024 * 1024),
        )(*results)

    wide, narrow = P("space", None, "chan", None), P(None, "chan", None)
    return jax.shard_map(
        shards,
        mesh=mesh,
        in_specs=(wide, wide, wide, narrow, narrow),
        out_specs=(wide, P(None, "chan", "space"), P(None, "chan", "space")),
        check_vma=False,
    )
```

time: 42.5 us -> 40.8 us (0.960)
  Pallas kernels: 41.8 us -> 40 us
    pallas_call x1, Pallas kernels: 41 us -> 39.2 us  [shards(): pl.pallas_call(functools.partial(kernel, (ns, nz, own, ny, scale, ends)),...]
where the time goes in v3:
time: 40.8 us; the launch traced here: 40.6 us
  Pallas kernels  40 us (98%)
  between operations  0.64 us (2%)
    pallas_call x1, Pallas kernels, shards(): pl.pallas_call(functools.partial(kernel, (ns, nz, own, ny, scale, ends)),...  39.2 us

profile of v3, /device:TPU:1, one launch (start us, length us, event | category | flops | bytes accessed | tf_op | source)
XLA Modules:
  0.0 40.6 jit_solution(13504242689723228908)
XLA Ops:
  0.6 39.2 %shard_map.76 = (bf16[1,16,16,128]{3,2,1,0:T(8,128)(2,1)S(1)}, f32[27,16,32]{2,1,0:T(8,128)S(1)}, f32[27,16,32]{2,1,0:T(8,128)S(1)}) custom-call(bf16[1,16,16,128]{3,2,1,0:T(8,128)(2,1)} %layer_hbm.1, bf16[1,16,16,128]{3,2,1,0:T(8,128)(2,1)} %pre_hbm.1, bf16[1,16,16,128]{3,2,1,0:T(8,128)(2,1)} %cot_hbm.1, bf16[27,16,256]{2,1,0:T(8,128)(2,1)} %w1_hbm.1, ...), custom_call_target="tpu_custom_call" | custom-call | tf_op jit(solution)/shard_map/pallas_call | solution.py:331
  39.8 0.8 %shard_map.77 = (bf16[1,16,16,128]{3,2,1,0:T(8,128)(2,1)}, f32[27,16,32]{2,1,0:T(8,128)}, f32[27,16,32]{2,1,0:T(8,128)}) custom-call(bf16[1,16,16,128]{3,2,1,0:T(8,128)(2,1)S(1)} %get-tuple-element.6.one_ref, f32[27,16,32]{2,1,0:T(8,128)S(1)} %get-tuple-element.7.two_ref, f32[27,16,32]{2,1,0:T(8,128)S(1)} %get-tuple-element.8.three_ref), custom_call_target="tpu_custom_call" | custom-call | tf_op jit(solution)/shard_map/pallas_call | solution.py:375

commit v4 on v3

--- a/solution.py
+++ b/solution.py
@@ -10,6 +10,9 @@
 MESH = pl.DeviceIdType.MESH
 OFFSETS = (-1, 0, 1)
 CHIPS = ((2, 2), (2, 0), (1, 2), (3, 2), (1, 0), (3, 0), (0, 2))
+
+
+DISTANCES = (2, 6, 1, 3, 5, 7, 4)
 
 
 def tap(a, b, c):
@@ -31,12 +34,14 @@
     out_ref, one_ref, two_ref,
     layer, pre, cot, w1, w2, hid, slope,
     got_cot, got_pre, cols_one, cols_two, prod, center,
-    part, send_part, recv_part, send_q, recv_q,
-    load_sem, gs, gr, fs, fr, hs, hr, qs, qr, ws, wr,
+    part, send_part, recv_part, near, line_sum, line_send, opposite, send_q, recv_q,
+    load_sem, gs, gr, fs, fr, hs, hr, qs, qr, ws, wr, ns_sem, nr_sem, os_sem, or_sem,
 ):
     ns, nz, own, ny, scale, (ends_one, ends_two, ends_three) = dims
     groups = got_cot.shape[0] // own
     rows = own * nz
+    line = ns // 2
+    taps = w1.shape[0]
     wide = part.shape[0] // ns
     s = lax.axis_index("space")
     c = lax.axis_index("chan")
@@ -197,7 +202,10 @@
             product(a)
             for z, value in plane_sum(a, first, last):
                 send_q[row, slot, z] = value.astype(jnp.bfloat16)
-        start_pair(pair)
+
+            @pl.when((s < ns - 1) if slot == 0 else (s > 0))
+            def _():
+                pair[slot].start()
         product(0)
         for z, value in plane_sum(0, first, last):
             center[z * own:(z + 1) * own, :] = value
@@ -222,7 +230,7 @@
 
     def weight_send(row):
         copies = []
-        for d in range(1, ns):
+        for d in DISTANCES:
             there = lax.rem(s + d, ns)
             block = pl.ds(pl.multiple_of(there * wide, wide), wide)
             copy = pltpu.make_async_remote_copy(
@@ -233,11 +241,53 @@
             copies.append(copy)
         return copies
 
+    side = lax.div(s, line)
+
+    def near_send():
+        copies = []
+        for d in (2, 1, 3):
+            place = lax.rem(s + d, line)
+            for e in range(2):
+                block = pl.ds(pl.multiple_of((e * line + place) * wide, wide), wide)
+                copies.append(pltpu.make_async_remote_copy(
+                    send_part.at[0, block], near.at[d - 1, e], ns_sem.at[d - 1, e], nr_sem.at[d - 1, e],
+                    device_id=(side * line + place, c), device_id_type=MESH,
+                ))
+        for copy in copies:
+            copy.start()
+        own_parts = [
+            part[pl.ds(pl.multiple_of((e * line + lax.rem(s, line)) * wide, wide), wide), :] for e in range(2)
+        ]
+        for e in range(2):
+            line_sum[e] = own_parts[e]
+        return copies
+
+    def across_send(copies):
+        for copy in copies:
+            copy.wait_recv()
+        for e in range(2):
+            total = line_sum[e]
+            for d in range(line - 1):
+                total = total + near[d, e].astype(jnp.float32)
+            line_sum[e] = total
+            line_send[e] = total.astype(jnp.bfloat16)
+        copy = pltpu.make_async_remote_copy(
+            line_send.at[1 - side], opposite, os_sem, or_sem,
+            device_id=((1 - side) * line + lax.rem(s, line), c), device_id_type=MESH,
+        )
+        copy.start()
+        return copy
+
+    def across_total(copy, ref):
+        copy.wait_recv()
+        total = line_sum[side] + opposite[...].astype(jnp.float32)
+        ref[...] = (total[:, :taps * own] * scale).T.reshape(ref.shape)
+
     def weight_total(total, copies, row, ref):
-        for d, copy in enumerate(copies):
+        for d, copy in zip(DISTANCES, copies):
             copy.wait_recv()
-            total = total + recv_part[row, d].astype(jnp.float32)
-        ref[...] = (total * scale).T.reshape(ref.shape)
+            total = total + recv_part[row, d - 1].astype(jnp.float32)
+        ref[...] = (total[:, :taps * own] * scale).T.reshape(ref.shape)
 
     chunks = len(ends_one)
     started = [start_gather(got_cot, 0, j, ends_one) for j in range(chunks)]
@@ -252,8 +302,8 @@
         (halo(hid.at[1], hid.at[0], 0, up), halo(hid.at[1], hid.at[2], 1, down)),
         (halo(layer.at[1], layer.at[0], 2, up), halo(layer.at[1], layer.at[2], 3, down)),
     ]
-    start_pair(halo_copies[0])
-    start_pair(halo_copies[1])
+    for cols in (cols_two, cols_one):
+        cols[taps * own:, :] = jnp.zeros((cols.shape[0] - taps * own, nz * ny), jnp.bfloat16)
     fill(cols_two, hid, 0)
     fill(cols_one, layer, 0)
     loads[3].wait()
@@ -263,6 +313,8 @@
     for j in range(chunks):
         pending += forward_gather(got_cot, 0, j, ends_one, *started[j])
         pairs.append(input_side(w2, got_cot, 0, j, ends_one, ends_two))
+    start_pair(halo_copies[0])
+    start_pair(halo_copies[1])
     started = []
     for j in range(chunks):
         first, last, grad = input_total(pairs[j], 0, j, ends_two)
@@ -274,7 +326,8 @@
     fill(cols_two, hid, -1)
     fill(cols_two, hid, 1)
     part[...] = weight_product(cols_two, got_cot, pl.ds(0, nz * ny))
-    total_two = weight_pack(0)
+    weight_pack(0)
+    near_copies = near_send()
 
     finish_pair(halo_copies[1], layer.at[0], layer.at[2])
     fill(cols_one, layer, -1)
@@ -282,21 +335,20 @@
 
     for j in range(chunks):
         pending += forward_gather(got_pre, 1, j, ends_two, *started[j])
-        if j == 0:
-            copies_two = weight_send(0)
         piece = weight_product(cols_one, got_pre, lanes(j, ends_two))
         part[...] = piece if j == 0 else part[...] + piece
         if j == chunks - 1:
             total_one = weight_pack(1)
             copies_one = weight_send(1)
         pairs.append(input_side(w1, got_pre, 1, j, ends_two, ends_three))
-    weight_total(total_two, copies_two, 0, two_ref)
+    across = across_send(near_copies)
     for j in range(chunks):
         first, last, grad = input_total(pairs[chunks + j], 1, j, ends_three)
         out_ref[0, first:last] = grad.astype(jnp.bfloat16).reshape(last - first, own, ny)
+    across_total(across, two_ref)
     weight_total(total_one, copies_one, 1, one_ref)
 
-    for copy in pending + copies_two + copies_one:
+    for copy in pending + near_copies + [across] + copies_one:
         copy.wait_send()
     for pair in halo_copies + pairs:
         sent_pair(pair)
@@ -319,6 +371,7 @@
     def shards(layer_input, pre_act, out_grad, weight_one, weight_two):
         _, nz, own, ny = layer_input.shape
         taps, _, chans = weight_one.shape
+        padded = -(-taps * own // 128) * 128
         scale = float(ns * ny * nz) ** -0.5
         chunks = 2
         ends = tuple(
@@ -347,13 +400,17 @@
                 pltpu.VMEM((nz * own, ny), f32),
                 pltpu.VMEM((chans, nz * ny), bf),
                 pltpu.VMEM((chans, nz * ny), bf),
-                pltpu.VMEM((taps * own, nz * ny), bf),
-                pltpu.VMEM((taps * own, nz * ny), bf),
+                pltpu.VMEM((padded, nz * ny), bf),
+                pltpu.VMEM((padded, nz * ny), bf),
                 pltpu.VMEM((taps * own, nz * ny), f32),
                 pltpu.VMEM((nz * own, ny), f32),
-                pltpu.VMEM((chans, taps * own), f32),
-                pltpu.VMEM((2, chans, taps * own), bf),
-                pltpu.VMEM((2, ns - 1, chans // ns, taps * own), bf),
+                pltpu.VMEM((chans, padded), f32),
+                pltpu.VMEM((2, chans, padded), bf),
+                pltpu.VMEM((2, ns - 1, chans // ns, padded), bf),
+                pltpu.VMEM((ns // 2 - 1, 2, chans // ns, padded), bf),
+                pltpu.VMEM((2, chans // ns, padded), f32),
+                pltpu.VMEM((2, chans // ns, padded), bf),
+                pltpu.VMEM((chans // ns, padded), bf),
                 pltpu.VMEM((2, 2, nz, own, ny), bf),
                 pltpu.VMEM((2, 2, nz, own, ny), bf),
                 dma((5,)),
@@ -367,6 +424,10 @@
                 dma((2, chunks, 2)),
                 dma((2, ns - 1)),
                 dma((2, ns - 1)),
+                dma((ns // 2 - 1, 2)),
+                dma((ns // 2 - 1, 2)),
+                dma,
+                dma,
             ],
             compiler_params=pltpu.CompilerParams(
                 collective_id=0, has_side_effects=True, vmem_limit_bytes=48 * 1024 * 1024

time: 40.8 us -> 39.7 us (0.973)
  Pallas kernels: 40 us -> 38.9 us
    pallas_call x1, Pallas kernels: 39.2 us -> 38.1 us  [shards(): pl.pallas_call(functools.partial(kernel, (ns, nz, own, ny, scale, ends)),...]
where the time goes in v4:
time: 39.7 us; the launch traced here: 39.6 us
  Pallas kernels  38.9 us (98%)
  between operations  0.64 us (2%)
    pallas_call x1, Pallas kernels, shards(): pl.pallas_call(functools.partial(kernel, (ns, nz, own, ny, scale, ends)),...  38.1 us
    pallas_call x1, Pallas kernels, shards(): pl.pallas_call(hand_out, out_shape=tuple((jax.ShapeDtypeStruct(v.shape, v...  0.81 us

profile of v4, /device:TPU:1, one launch (start us, length us, event | category | flops | bytes accessed | tf_op | source)
XLA Modules:
  0.0 39.6 jit_solution(17809548452296427061)
XLA Ops:
  0.6 38.1 %shard_map.76 = (bf16[1,16,16,128]{3,2,1,0:T(8,128)(2,1)S(1)}, f32[27,16,32]{2,1,0:T(8,128)S(1)}, f32[27,16,32]{2,1,0:T(8,128)S(1)}) custom-call(bf16[1,16,16,128]{3,2,1,0:T(8,128)(2,1)} %layer_hbm.1, bf16[1,16,16,128]{3,2,1,0:T(8,128)(2,1)} %pre_hbm.1, bf16[1,16,16,128]{3,2,1,0:T(8,128)(2,1)} %cot_hbm.1, bf16[27,16,256]{2,1,0:T(8,128)(2,1)} %w1_hbm.1, ...), custom_call_target="tpu_custom_call" | custom-call | tf_op jit(solution)/shard_map/pallas_call | solution.py:384
  38.8 0.8 %shard_map.77 = (bf16[1,16,16,128]{3,2,1,0:T(8,128)(2,1)}, f32[27,16,32]{2,1,0:T(8,128)}, f32[27,16,32]{2,1,0:T(8,128)}) custom-call(bf16[1,16,16,128]{3,2,1,0:T(8,128)(2,1)S(1)} %get-tuple-element.6.one_ref, f32[27,16,32]{2,1,0:T(8,128)S(1)} %get-tuple-element.7.two_ref, f32[27,16,32]{2,1,0:T(8,128)S(1)} %get-tuple-element.8.three_ref), custom_call_target="tpu_custom_call" | custom-call | tf_op jit(solution)/shard_map/pallas_call | solution.py:436

commit v5 on v4

--- a/solution.py
+++ b/solution.py
@@ -12,6 +12,7 @@
 CHIPS = ((2, 2), (2, 0), (1, 2), (3, 2), (1, 0), (3, 0), (0, 2))
 
 
+GROUPS = (0, 3, 1, 2)
 DISTANCES = (2, 6, 1, 3, 5, 7, 4)
 
 
@@ -32,7 +33,7 @@
     dims,
     layer_hbm, pre_hbm, cot_hbm, w1_hbm, w2_hbm,
     out_ref, one_ref, two_ref,
-    layer, pre, cot, w1, w2, hid, slope,
+    layer, pre, cot, w1, w2, ordered_one, ordered_two, hid, slope,
     got_cot, got_pre, cols_one, cols_two, prod, center,
     part, send_part, recv_part, near, line_sum, line_send, opposite, send_q, recv_q,
     load_sem, gs, gr, fs, fr, hs, hr, qs, qr, ws, wr, ns_sem, nr_sem, os_sem, or_sem,
@@ -42,7 +43,6 @@
     rows = own * nz
     line = ns // 2
     taps = w1.shape[0]
-    wide = part.shape[0] // ns
     s = lax.axis_index("space")
     c = lax.axis_index("chan")
     zc, wc = lax.div(c, 4), lax.rem(c, 4)
@@ -52,7 +52,8 @@
         return lax.rem(zc + dz, levels) * 4 + (wc ^ dw)
 
     sibling = (s, c ^ 1)
-    mine = pl.ds(pl.multiple_of(c * own, own), own)
+    core, half = lax.rem(c, 2), got_cot.shape[0] // 2
+    mine = pl.ds(pl.multiple_of(core * half + lax.div(c, 2) * own, own), own)
 
     barrier = pltpu.get_barrier_semaphore()
     partners = [(s, chip(*d)) for d in CHIPS] + [(lax.rem(s + d, ns), c) for d in range(1, ns)] + [sibling]
@@ -87,29 +88,36 @@
             )
             copy.start()
             sends.append(copy)
-        home = pltpu.make_async_remote_copy(
-            buf.at[mine, span], buf.at[mine, span], fs.at[row, j, len(CHIPS)], fr.at[row, j, len(CHIPS)],
-            device_id=sibling, device_id_type=MESH,
-        )
-        home.start()
-        return home, sends
-
-    def forward_gather(buf, row, j, ends, home, sends):
+        return sends
+
+    def forward_gather(buf, row, j, ends, sends):
         span = lanes(j, ends)
         passed = []
-        for k in reversed(range(len(CHIPS))):
-            dz, dw = CHIPS[k]
-            sends[k].wait_recv()
-            origin = pl.ds(pl.multiple_of(chip(levels - dz, dw) * own, own), own)
+        for g in GROUPS:
+            for k, (dz, _) in enumerate(CHIPS):
+                if (dz + g) % levels == 0:
+                    sends[k].wait_recv()
+            block = pl.ds(pl.multiple_of(core * half + lax.rem(zc + g, levels) * (2 * own), own), 2 * own)
             copy = pltpu.make_async_remote_copy(
-                buf.at[origin, span], buf.at[origin, span], fs.at[row, j, k], fr.at[row, j, k],
+                buf.at[block, span], buf.at[block, span], fs.at[row, j, g], fr.at[row, j, g],
                 device_id=sibling, device_id_type=MESH,
             )
             copy.start()
             passed.append(copy)
-        for copy in [home] + passed:
+        for copy in passed:
             copy.wait_recv()
-        return [home] + passed + sends
+        return passed + sends
+
+    def permuted(weight, ordered):
+        source = lax.broadcasted_iota(jnp.int32, (2 * half, 2 * half), 0)
+        lane = lax.broadcasted_iota(jnp.int32, (1, 2 * half), 1)
+        parity = jnp.where(lane < half, 0, 1)
+        inner = lane - parity * half
+        target = lax.div(inner, own) * (2 * own) + parity * own + lax.rem(inner, own)
+        pick = jnp.where(source == target, 1.0, 0.0).astype(jnp.bfloat16)
+        ordered[...] = jnp.dot(
+            weight[...].reshape(taps * own, 2 * half), pick, preferred_element_type=jnp.float32
+        ).astype(jnp.bfloat16)
 
     def halo(src, dst, sem, there):
         return pltpu.make_async_remote_copy(
@@ -187,7 +195,7 @@
 
         def product(a):
             lo = tap(a, -1, -1) * own
-            left = weight[9 * (a + 1):9 * (a + 2)].reshape(9 * own, groups * own)
+            left = weight[lo:lo + 9 * own, :]
             prod[lo:lo + 9 * own, span] = jnp.dot(left, field, preferred_element_type=jnp.float32)
 
         def copy(slot, there):
@@ -220,21 +228,25 @@
         return first, last, center[first * own:last * own, :] + low + high
 
     def weight_product(cols, got, span):
-        return lax.dot_general(
+        value = lax.dot_general(
             got[:, span], cols[:, span], (((1,), (1,)), ((), ())), preferred_element_type=jnp.float32
         )
+        return value.reshape(part.shape)
+
+    def block_of(index):
+        return pl.ds(pl.multiple_of(index * own, own), own)
 
     def weight_pack(row):
         send_part[row] = part[...].astype(jnp.bfloat16)
-        return part[pl.ds(pl.multiple_of(s * wide, wide), wide), :]
+        return part[:, block_of(s), :]
 
     def weight_send(row):
         copies = []
         for d in DISTANCES:
             there = lax.rem(s + d, ns)
-            block = pl.ds(pl.multiple_of(there * wide, wide), wide)
+            block = block_of(there)
             copy = pltpu.make_async_remote_copy(
-                send_part.at[row, block], recv_part.at[row, d - 1], ws.at[row, d - 1], wr.at[row, d - 1],
+                send_part.at[row, :, block], recv_part.at[row, d - 1], ws.at[row, d - 1], wr.at[row, d - 1],
                 device_id=(there, c), device_id_type=MESH,
             )
             copy.start()
@@ -248,15 +260,15 @@
         for d in (2, 1, 3):
             place = lax.rem(s + d, line)
             for e in range(2):
-                block = pl.ds(pl.multiple_of((e * line + place) * wide, wide), wide)
+                block = block_of(e * line + place)
                 copies.append(pltpu.make_async_remote_copy(
-                    send_part.at[0, block], near.at[d - 1, e], ns_sem.at[d - 1, e], nr_sem.at[d - 1, e],
+                    send_part.at[0, :, block], near.at[d - 1, e], ns_sem.at[d - 1, e], nr_sem.at[d - 1, e],
                     device_id=(side * line + place, c), device_id_type=MESH,
                 ))
         for copy in copies:
             copy.start()
         own_parts = [
-            part[pl.ds(pl.multiple_of((e * line + lax.rem(s, line)) * wide, wide), wide), :] for e in range(2)
+            part[:, block_of(e * line + lax.rem(s, line)), :] for e in range(2)
         ]
         for e in range(2):
             line_sum[e] = own_parts[e]
@@ -281,13 +293,13 @@
     def across_total(copy, ref):
         copy.wait_recv()
         total = line_sum[side] + opposite[...].astype(jnp.float32)
-        ref[...] = (total[:, :taps * own] * scale).T.reshape(ref.shape)
+        ref[...] = (total.reshape(2 * own, -1)[:, :taps * own] * scale).T.reshape(ref.shape)
 
     def weight_total(total, copies, row, ref):
         for d, copy in zip(DISTANCES, copies):
             copy.wait_recv()
             total = total + recv_part[row, d - 1].astype(jnp.float32)
-        ref[...] = (total[:, :taps * own] * scale).T.reshape(ref.shape)
+        ref[...] = (total.reshape(2 * own, -1)[:, :taps * own] * scale).T.reshape(ref.shape)
 
     chunks = len(ends_one)
     started = [start_gather(got_cot, 0, j, ends_one) for j in range(chunks)]
@@ -307,12 +319,14 @@
     fill(cols_two, hid, 0)
     fill(cols_one, layer, 0)
     loads[3].wait()
+    permuted(w2, ordered_two)
     loads[4].wait()
+    permuted(w1, ordered_one)
 
     pending, pairs = [], []
     for j in range(chunks):
-        pending += forward_gather(got_cot, 0, j, ends_one, *started[j])
-        pairs.append(input_side(w2, got_cot, 0, j, ends_one, ends_two))
+        pending += forward_gather(got_cot, 0, j, ends_one, started[j])
+        pairs.append(input_side(ordered_two, got_cot, 0, j, ends_one, ends_two))
     start_pair(halo_copies[0])
     start_pair(halo_copies[1])
     started = []
@@ -334,24 +348,27 @@
     fill(cols_one, layer, 1)
 
     for j in range(chunks):
-        pending += forward_gather(got_pre, 1, j, ends_two, *started[j])
+        pending += forward_gather(got_pre, 1, j, ends_two, started[j])
         piece = weight_product(cols_one, got_pre, lanes(j, ends_two))
         part[...] = piece if j == 0 else part[...] + piece
         if j == chunks - 1:
             total_one = weight_pack(1)
             copies_one = weight_send(1)
-        pairs.append(input_side(w1, got_pre, 1, j, ends_two, ends_three))
+        pairs.append(input_side(ordered_one, got_pre, 1, j, ends_two, ends_three))
     across = across_send(near_copies)
+    for copy in pending + near_copies:
+        copy.wait_send()
+    for pair in halo_copies + pairs[:chunks]:
+        sent_pair(pair)
     for j in range(chunks):
         first, last, grad = input_total(pairs[chunks + j], 1, j, ends_three)
         out_ref[0, first:last] = grad.astype(jnp.bfloat16).reshape(last - first, own, ny)
     across_total(across, two_ref)
+    for copy in [across] + copies_one:
+        copy.wait_send()
+    for pair in pairs[chunks:]:
+        sent_pair(pair)
     weight_total(total_one, copies_one, 1, one_ref)
-
-    for copy in pending + near_copies + [across] + copies_one:
-        copy.wait_send()
-    for pair in halo_copies + pairs:
-        sent_pair(pair)
 
 
 def hand_out(one_ref, two_ref, three_ref, one_out, two_out, three_out, sem):
@@ -396,6 +413,8 @@
                 pltpu.VMEM((nz, own, ny), bf),
                 pltpu.VMEM(weight_one.shape, bf),
                 pltpu.VMEM(weight_two.shape, bf),
+                pltpu.VMEM((taps * own, chans), bf),
+                pltpu.VMEM((taps * own, chans), bf),
                 pltpu.VMEM((3, nz, own, ny), bf),
                 pltpu.VMEM((nz * own, ny), f32),
                 pltpu.VMEM((chans, nz * ny), bf),
@@ -404,20 +423,20 @@
                 pltpu.VMEM((padded, nz * ny), bf),
                 pltpu.VMEM((taps * own, nz * ny), f32),
                 pltpu.VMEM((nz * own, ny), f32),
-                pltpu.VMEM((chans, padded), f32),
-                pltpu.VMEM((2, chans, padded), bf),
-                pltpu.VMEM((2, ns - 1, chans // ns, padded), bf),
-                pltpu.VMEM((ns // 2 - 1, 2, chans // ns, padded), bf),
-                pltpu.VMEM((2, chans // ns, padded), f32),
-                pltpu.VMEM((2, chans // ns, padded), bf),
-                pltpu.VMEM((chans // ns, padded), bf),
+                pltpu.VMEM((2, chans // 2, padded), f32),
+                pltpu.VMEM((2, 2, chans // 2, padded), bf),
+                pltpu.VMEM((2, ns - 1, 2, own, padded), bf),
+                pltpu.VMEM((ns // 2 - 1, 2, 2, own, padded), bf),
+                pltpu.VMEM((2, 2, own, padded), f32),
+                pltpu.VMEM((2, 2, own, padded), bf),
+                pltpu.VMEM((2, own, padded), bf),
                 pltpu.VMEM((2, 2, nz, own, ny), bf),
                 pltpu.VMEM((2, 2, nz, own, ny), bf),
                 dma((5,)),
                 dma((2, chunks, len(CHIPS))),
                 dma((2, chunks, len(CHIPS))),
-                dma((2, chunks, len(CHIPS) + 1)),
-                dma((2, chunks, len(CHIPS) + 1)),
+                dma((2, chunks, len(GROUPS))),
+                dma((2, chunks, len(GROUPS))),
                 dma((4,)),
                 dma((4,)),
                 dma((2, chunks, 2)),

time: 39.7 us -> 39.4 us (level)
  Pallas kernels: 38.9 us -> 38.3 us
    pallas_call x1, Pallas kernels: 38.1 us -> 37.5 us  [shards(): pl.pallas_call(functools.partial(kernel, (ns, nz, own, ny, scale, ends)),...]
where the time goes in v5:
time: 39.4 us; the launch traced here: 39 us
  Pallas kernels  38.3 us (97%)
  between operations  0.64 us (2%)
    pallas_call x1, Pallas kernels, shards(): pl.pallas_call(functools.partial(kernel, (ns, nz, own, ny, scale, ends)),...  37.5 us
    pallas_call x1, Pallas kernels, shards(): pl.pallas_call(hand_out, out_shape=tuple((jax.ShapeDtypeStruct(v.shape, v...  0.81 us

profile of v5, /device:TPU:1, one launch (start us, length us, event | category | flops | bytes accessed | tf_op | source)
XLA Modules:
  0.0 39.0 jit_solution(15587785028595779736)
XLA Ops:
  0.6 37.5 %shard_map.76 = (bf16[1,16,16,128]{3,2,1,0:T(8,128)(2,1)S(1)}, f32[27,16,32]{2,1,0:T(8,128)S(1)}, f32[27,16,32]{2,1,0:T(8,128)S(1)}) custom-call(bf16[1,16,16,128]{3,2,1,0:T(8,128)(2,1)} %layer_hbm.1, bf16[1,16,16,128]{3,2,1,0:T(8,128)(2,1)} %pre_hbm.1, bf16[1,16,16,128]{3,2,1,0:T(8,128)(2,1)} %cot_hbm.1, bf16[27,16,256]{2,1,0:T(8,128)(2,1)} %w1_hbm.1, ...), custom_call_target="tpu_custom_call" | custom-call | tf_op jit(solution)/shard_map/pallas_call | solution.py:401
  38.1 0.8 %shard_map.77 = (bf16[1,16,16,128]{3,2,1,0:T(8,128)(2,1)}, f32[27,16,32]{2,1,0:T(8,128)}, f32[27,16,32]{2,1,0:T(8,128)}) custom-call(bf16[1,16,16,128]{3,2,1,0:T(8,128)(2,1)S(1)} %get-tuple-element.6.one_ref, f32[27,16,32]{2,1,0:T(8,128)S(1)} %get-tuple-element.7.two_ref, f32[27,16,32]{2,1,0:T(8,128)S(1)} %get-tuple-element.8.three_ref), custom_call_target="tpu_custom_call" | custom-call | tf_op jit(solution)/shard_map/pallas_call | solution.py:455

commit v6 on v5

--- a/solution.py
+++ b/solution.py
@@ -104,9 +104,7 @@
             )
             copy.start()
             passed.append(copy)
-        for copy in passed:
-            copy.wait_recv()
-        return passed + sends
+        return passed, sends
 
     def permuted(weight, ordered):
         source = lax.broadcasted_iota(jnp.int32, (2 * half, 2 * half), 0)
@@ -236,18 +234,21 @@
     def block_of(index):
         return pl.ds(pl.multiple_of(index * own, own), own)
 
-    def weight_pack(row):
-        send_part[row] = part[...].astype(jnp.bfloat16)
-        return part[:, block_of(s), :]
-
-    def weight_send(row):
+    def weight_half(parity, span, add):
+        strip = pl.ds(pl.multiple_of(parity * half, half), half)
+        piece = lax.dot_general(
+            got_pre[strip, span], cols_one[:, span], (((1,), (1,)), ((), ())), preferred_element_type=jnp.float32
+        )
+        part[parity] = part[parity] + piece if add else piece
+
+    def half_send(turn, parity):
+        send_part[1, parity] = part[parity].astype(jnp.bfloat16)
         copies = []
         for d in DISTANCES:
             there = lax.rem(s + d, ns)
-            block = block_of(there)
             copy = pltpu.make_async_remote_copy(
-                send_part.at[row, :, block], recv_part.at[row, d - 1], ws.at[row, d - 1], wr.at[row, d - 1],
-                device_id=(there, c), device_id_type=MESH,
+                send_part.at[1, parity, block_of(there)], recv_part.at[d - 1, parity],
+                ws.at[turn, d - 1], wr.at[turn, d - 1], device_id=(there, c), device_id_type=MESH,
             )
             copy.start()
             copies.append(copy)
@@ -295,10 +296,12 @@
         total = line_sum[side] + opposite[...].astype(jnp.float32)
         ref[...] = (total.reshape(2 * own, -1)[:, :taps * own] * scale).T.reshape(ref.shape)
 
-    def weight_total(total, copies, row, ref):
-        for d, copy in zip(DISTANCES, copies):
+    def weight_total(copies, ref):
+        for copy in copies:
             copy.wait_recv()
-            total = total + recv_part[row, d - 1].astype(jnp.float32)
+        total = part[:, block_of(s), :]
+        for d in range(ns - 1):
+            total = total + recv_part[d].astype(jnp.float32)
         ref[...] = (total.reshape(2 * own, -1)[:, :taps * own] * scale).T.reshape(ref.shape)
 
     chunks = len(ends_one)
@@ -325,7 +328,10 @@
 
     pending, pairs = [], []
     for j in range(chunks):
-        pending += forward_gather(got_cot, 0, j, ends_one, started[j])
+        passed, sends = forward_gather(got_cot, 0, j, ends_one, started[j])
+        for copy in passed:
+            copy.wait_recv()
+        pending += passed + sends
         pairs.append(input_side(ordered_two, got_cot, 0, j, ends_one, ends_two))
     start_pair(halo_copies[0])
     start_pair(halo_copies[1])
@@ -340,20 +346,24 @@
     fill(cols_two, hid, -1)
     fill(cols_two, hid, 1)
     part[...] = weight_product(cols_two, got_cot, pl.ds(0, nz * ny))
-    weight_pack(0)
+    send_part[0] = part[...].astype(jnp.bfloat16)
     near_copies = near_send()
 
     finish_pair(halo_copies[1], layer.at[0], layer.at[2])
     fill(cols_one, layer, -1)
     fill(cols_one, layer, 1)
 
+    copies_one = []
     for j in range(chunks):
-        pending += forward_gather(got_pre, 1, j, ends_two, started[j])
-        piece = weight_product(cols_one, got_pre, lanes(j, ends_two))
-        part[...] = piece if j == 0 else part[...] + piece
-        if j == chunks - 1:
-            total_one = weight_pack(1)
-            copies_one = weight_send(1)
+        passed, sends = forward_gather(got_pre, 1, j, ends_two, started[j])
+        for turn, parity in enumerate((core, 1 - core)):
+            if turn:
+                for copy in passed:
+                    copy.wait_recv()
+            weight_half(parity, lanes(j, ends_two), j > 0)
+            if j == chunks - 1:
+                copies_one += half_send(turn, parity)
+        pending += passed + sends
         pairs.append(input_side(ordered_one, got_pre, 1, j, ends_two, ends_three))
     across = across_send(near_copies)
     for copy in pending + near_copies:
@@ -368,7 +378,7 @@
         copy.wait_send()
     for pair in pairs[chunks:]:
         sent_pair(pair)
-    weight_total(total_one, copies_one, 1, one_ref)
+    weight_total(copies_one, one_ref)
 
 
 def hand_out(one_ref, two_ref, three_ref, one_out, two_out, three_out, sem):
@@ -425,7 +435,7 @@
                 pltpu.VMEM((nz * own, ny), f32),
                 pltpu.VMEM((2, chans // 2, padded), f32),
                 pltpu.VMEM((2, 2, chans // 2, padded), bf),
-                pltpu.VMEM((2, ns - 1, 2, own, padded), bf),
+                pltpu.VMEM((ns - 1, 2, own, padded), bf),
                 pltpu.VMEM((ns // 2 - 1, 2, 2, own, padded), bf),
                 pltpu.VMEM((2, 2, own, padded), f32),
                 pltpu.VMEM((2, 2, own, padded), bf),

time: 39.4 us -> 38.8 us (0.985)
  Pallas kernels: 38.3 us -> 37.9 us
where the time goes in v6:
time: 38.8 us; the launch traced here: 38.6 us
  Pallas kernels  37.9 us (98%)
  between operations  0.64 us (2%)
    pallas_call x1, Pallas kernels, shards(): pl.pallas_call(functools.partial(kernel, (ns, nz, own, ny, scale, ends)),...  37.1 us
    pallas_call x1, Pallas kernels, shards(): pl.pallas_call(hand_out, out_shape=tuple((jax.ShapeDtypeStruct(v.shape, v...  0.81 us

profile of v6, /device:TPU:1, one launch (start us, length us, event | category | flops | bytes accessed | tf_op | source)
XLA Modules:
  0.0 38.6 jit_solution(17423384549977178131)
XLA Ops:
  0.6 37.1 %shard_map.76 = (bf16[1,16,16,128]{3,2,1,0:T(8,128)(2,1)S(1)}, f32[27,16,32]{2,1,0:T(8,128)S(1)}, f32[27,16,32]{2,1,0:T(8,128)S(1)}) custom-call(bf16[1,16,16,128]{3,2,1,0:T(8,128)(2,1)} %layer_hbm.1, bf16[1,16,16,128]{3,2,1,0:T(8,128)(2,1)} %pre_hbm.1, bf16[1,16,16,128]{3,2,1,0:T(8,128)(2,1)} %cot_hbm.1, bf16[27,16,256]{2,1,0:T(8,128)(2,1)} %w1_hbm.1, ...), custom_call_target="tpu_custom_call" | custom-call | tf_op jit(solution)/shard_map/pallas_call | solution.py:411
  37.8 0.8 %shard_map.77 = (bf16[1,16,16,128]{3,2,1,0:T(8,128)(2,1)}, f32[27,16,32]{2,1,0:T(8,128)}, f32[27,16,32]{2,1,0:T(8,128)}) custom-call(bf16[1,16,16,128]{3,2,1,0:T(8,128)(2,1)S(1)} %get-tuple-element.6.one_ref, f32[27,16,32]{2,1,0:T(8,128)S(1)} %get-tuple-element.7.two_ref, f32[27,16,32]{2,1,0:T(8,128)S(1)} %get-tuple-element.8.three_ref), custom_call_target="tpu_custom_call" | custom-call | tf_op jit(solution)/shard_map/pallas_call | solution.py:465

commit v7 on v6

--- a/solution.py
+++ b/solution.py
@@ -333,7 +333,8 @@
             copy.wait_recv()
         pending += passed + sends
         pairs.append(input_side(ordered_two, got_cot, 0, j, ends_one, ends_two))
-    start_pair(halo_copies[0])
+        if j == 0:
+            start_pair(halo_copies[0])
     start_pair(halo_copies[1])
     started = []
     for j in range(chunks):

time: 38.8 us -> 38.5 us (level)
  no operation moved by 1% of the time
where the time goes in v7:
time: 38.5 us; the launch traced here: 38.4 us
  Pallas kernels  37.8 us (98%)
  between operations  0.64 us (2%)
    pallas_call x1, Pallas kernels, shards(): pl.pallas_call(functools.partial(kernel, (ns, nz, own, ny, scale, ends)),...  37 us
    pallas_call x1, Pallas kernels, shards(): pl.pallas_call(hand_out, out_shape=tuple((jax.ShapeDtypeStruct(v.shape, v...  0.81 us

profile of v7, /device:TPU:1, one launch (start us, length us, event | category | flops | bytes accessed | tf_op | source)
XLA Modules:
  0.0 38.4 jit_solution(10869194616745518988)
XLA Ops:
  0.6 37.0 %shard_map.76 = (bf16[1,16,16,128]{3,2,1,0:T(8,128)(2,1)S(1)}, f32[27,16,32]{2,1,0:T(8,128)S(1)}, f32[27,16,32]{2,1,0:T(8,128)S(1)}) custom-call(bf16[1,16,16,128]{3,2,1,0:T(8,128)(2,1)} %layer_hbm.1, bf16[1,16,16,128]{3,2,1,0:T(8,128)(2,1)} %pre_hbm.1, bf16[1,16,16,128]{3,2,1,0:T(8,128)(2,1)} %cot_hbm.1, bf16[27,16,256]{2,1,0:T(8,128)(2,1)} %w1_hbm.1, ...), custom_call_target="tpu_custom_call" | custom-call | tf_op jit(solution)/shard_map/pallas_call | solution.py:412
  37.6 0.8 %shard_map.77 = (bf16[1,16,16,128]{3,2,1,0:T(8,128)(2,1)}, f32[27,16,32]{2,1,0:T(8,128)}, f32[27,16,32]{2,1,0:T(8,128)}) custom-call(bf16[1,16,16,128]{3,2,1,0:T(8,128)(2,1)S(1)} %get-tuple-element.6.one_ref, f32[27,16,32]{2,1,0:T(8,128)S(1)} %get-tuple-element.7.two_ref, f32[27,16,32]{2,1,0:T(8,128)S(1)} %get-tuple-element.8.three_ref), custom_call_target="tpu_custom_call" | custom-call | tf_op jit(solution)/shard_map/pallas_call | solution.py:466

commit v8 on v7

--- a/solution.py
+++ b/solution.py
@@ -365,8 +365,9 @@
             if j == chunks - 1:
                 copies_one += half_send(turn, parity)
         pending += passed + sends
+        if j == chunks - 1:
+            across = across_send(near_copies)
         pairs.append(input_side(ordered_one, got_pre, 1, j, ends_two, ends_three))
-    across = across_send(near_copies)
     for copy in pending + near_copies:
         copy.wait_send()
     for pair in halo_copies + pairs[:chunks]:

time: 38.5 us -> 38.5 us (level)
  no operation moved by 1% of the time
where the time goes in v8:
time: 38.5 us; the launch traced here: 38.4 us
  Pallas kernels  37.7 us (98%)
  between operations  0.64 us (2%)
    pallas_call x1, Pallas kernels, shards(): pl.pallas_call(functools.partial(kernel, (ns, nz, own, ny, scale, ends)),...  36.9 us
    pallas_call x1, Pallas kernels, shards(): pl.pallas_call(hand_out, out_shape=tuple((jax.ShapeDtypeStruct(v.shape, v...  0.81 us

profile of v8, /device:TPU:1, one launch (start us, length us, event | category | flops | bytes accessed | tf_op | source)
XLA Modules:
  0.0 38.4 jit_solution(8766290873642014448)
XLA Ops:
  0.6 36.9 %shard_map.76 = (bf16[1,16,16,128]{3,2,1,0:T(8,128)(2,1)S(1)}, f32[27,16,32]{2,1,0:T(8,128)S(1)}, f32[27,16,32]{2,1,0:T(8,128)S(1)}) custom-call(bf16[1,16,16,128]{3,2,1,0:T(8,128)(2,1)} %layer_hbm.1, bf16[1,16,16,128]{3,2,1,0:T(8,128)(2,1)} %pre_hbm.1, bf16[1,16,16,128]{3,2,1,0:T(8,128)(2,1)} %cot_hbm.1, bf16[27,16,256]{2,1,0:T(8,128)(2,1)} %w1_hbm.1, ...), custom_call_target="tpu_custom_call" | custom-call | tf_op jit(solution)/shard_map/pallas_call | solution.py:413
  37.6 0.8 %shard_map.77 = (bf16[1,16,16,128]{3,2,1,0:T(8,128)(2,1)}, f32[27,16,32]{2,1,0:T(8,128)}, f32[27,16,32]{2,1,0:T(8,128)}) custom-call(bf16[1,16,16,128]{3,2,1,0:T(8,128)(2,1)S(1)} %get-tuple-element.6.one_ref, f32[27,16,32]{2,1,0:T(8,128)S(1)} %get-tuple-element.7.two_ref, f32[27,16,32]{2,1,0:T(8,128)S(1)} %get-tuple-element.8.three_ref), custom_call_target="tpu_custom_call" | custom-call | tf_op jit(solution)/shard_map/pallas_call | solution.py:467

commit v9 on v8

--- a/solution.py
+++ b/solution.py
@@ -12,7 +12,7 @@
 CHIPS = ((2, 2), (2, 0), (1, 2), (3, 2), (1, 0), (3, 0), (0, 2))
 
 
-GROUPS = (0, 3, 1, 2)
+GROUPS = (3, 1, 0, 2)
 DISTANCES = (2, 6, 1, 3, 5, 7, 4)
 
 

time: 38.5 us -> 38.6 us (level)
  no operation moved by 1% of the time
where the time goes in v9:
time: 38.6 us; the launch traced here: 38.5 us
  Pallas kernels  37.8 us (98%)
  between operations  0.64 us (2%)
    pallas_call x1, Pallas kernels, shards(): pl.pallas_call(functools.partial(kernel, (ns, nz, own, ny, scale, ends)),...  37 us
    pallas_call x1, Pallas kernels, shards(): pl.pallas_call(hand_out, out_shape=tuple((jax.ShapeDtypeStruct(v.shape, v...  0.81 us

profile of v9, /device:TPU:1, one launch (start us, length us, event | category | flops | bytes accessed | tf_op | source)
XLA Modules:
  0.0 38.5 jit_solution(15903057213243398276)
XLA Ops:
  0.6 37.0 %shard_map.76 = (bf16[1,16,16,128]{3,2,1,0:T(8,128)(2,1)S(1)}, f32[27,16,32]{2,1,0:T(8,128)S(1)}, f32[27,16,32]{2,1,0:T(8,128)S(1)}) custom-call(bf16[1,16,16,128]{3,2,1,0:T(8,128)(2,1)} %layer_hbm.1, bf16[1,16,16,128]{3,2,1,0:T(8,128)(2,1)} %pre_hbm.1, bf16[1,16,16,128]{3,2,1,0:T(8,128)(2,1)} %cot_hbm.1, bf16[27,16,256]{2,1,0:T(8,128)(2,1)} %w1_hbm.1, ...), custom_call_target="tpu_custom_call" | custom-call | tf_op jit(solution)/shard_map/pallas_call | solution.py:413
  37.7 0.8 %shard_map.77 = (bf16[1,16,16,128]{3,2,1,0:T(8,128)(2,1)}, f32[27,16,32]{2,1,0:T(8,128)}, f32[27,16,32]{2,1,0:T(8,128)}) custom-call(bf16[1,16,16,128]{3,2,1,0:T(8,128)(2,1)S(1)} %get-tuple-element.6.one_ref, f32[27,16,32]{2,1,0:T(8,128)S(1)} %get-tuple-element.7.two_ref, f32[27,16,32]{2,1,0:T(8,128)S(1)} %get-tuple-element.8.three_ref), custom_call_target="tpu_custom_call" | custom-call | tf_op jit(solution)/shard_map/pallas_call | solution.py:467
